TPU v7x, 256 devices: a whole 4x4x8 slice. The times are simulated.
256 devices in a mesh: dp: 32 (over x, y, core), mp: 8 (over z).
Axes of the slice: x: 4, y: 4, z: 8, core: 2. Of those that a mesh axis runs over, the one named last changes fastest.
Arguments:
- queries: bfloat16 [16384, 5120], P(('dp', 'mp')), may hold values from -22 to 22
- keys: bfloat16 [16384, 1024], P(('dp', 'mp')), may hold values from -6 to 6
- values: bfloat16 [16384, 1024], P(('dp', 'mp')), may hold values from -12 to 12
- prefix_keys: bfloat16 [32, 2048, 1024], P('dp', None, 'mp'), may hold values from -6 to 6
- prefix_values: bfloat16 [32, 2048, 1024], P('dp', None, 'mp'), may hold values from -12 to 12
- prompt_of: int32 [64], P('dp'), may hold values from 0 to 31, as said below
- lengths: int32 [64], P('dp'), may hold values from 32 to 256, as said below
- cotangent: bfloat16 [16384, 5120], P(('dp', 'mp')), may hold values from -20 to 20
Outputs:
- attended: bfloat16 [16384, 5120], P(('dp', 'mp'))
- d_queries: bfloat16 [16384, 5120], P(('dp', 'mp'))
- d_keys: bfloat16 [16384, 1024], P(('dp', 'mp'))
- d_values: bfloat16 [16384, 1024], P(('dp', 'mp'))
- d_prefix_keys: bfloat16 [32, 2048, 1024], P('dp', None, 'mp')
- d_prefix_values: bfloat16 [32, 2048, 1024], P('dp', None, 'mp')
Inputs may be any that keep to these rules, and one draw needn't show every extreme that they name: `prompt_of`: prompt p is held at dp index p. The completions at dp index d (completions d * 2 to d * 2 + 1) belong to prompts max(d - 3, 0) to d; at some position r among them the completion belongs to prompt d - (d % 4), and the one at position (r + 1) % 2 belongs to prompt d. `lengths`: at least one completion has 256 live tokens.
All inputs are finite; a program needn't handle non-finite values.
Results may differ from a plain program's by a relative error of at most 0.012.
The roundings to bfloat16 on the way count: a program that leaves them out, or rounds other values in their place, can miss the bound.
Values may be sent and summed in bfloat16 or wider, within the bound.
No kernel may reach another device: no remote copies, remote signals or barrier semaphores. Data moves between devices by JAX's collectives and lax.ppermute only.
A program may use at most 128 MiB of HBM per device.

v0:
```python
import jax
import jax.numpy as jnp
from jax import lax
from jax.sharding import PartitionSpec as P

HD = 128
REACH = 4


masked_score = -1e30


def shifted(shard, axis, by):
    devices = lax.axis_size(axis)
    pairs = [(i, i + by) for i in range(devices) if 0 <= i + by < devices]
    return lax.ppermute(shard, axis, pairs)


def attend_block(inputs):
    query_rows, key_rows, value_rows, grad_rows, prefix_pair, length = inputs
    clen = query_rows.shape[0]
    prefix = prefix_pair.shape[1]
    kv_local = key_rows.shape[1]
    head_dim = query_rows.shape[-1]
    scale = head_dim ** (-0.5)
    all_keys = jnp.concatenate([prefix_pair[0].reshape(prefix, kv_local, head_dim), key_rows], 0)
    all_values = jnp.concatenate(
        [prefix_pair[1].reshape(prefix, kv_local, head_dim), value_rows], 0
    )
    scores = (
        jnp.einsum("tkgd,skd->kgts", query_rows, all_keys, preferred_element_type=jnp.float32)
        * scale
    )
    positions = jnp.arange(clen, dtype=jnp.int32)
    key_pos = jnp.arange(prefix + clen, dtype=jnp.int32) - prefix
    allowed = (key_pos[None, :] < 0) | (key_pos[None, :] <= positions[:, None]) & (
        key_pos[None, :] < length
    )
    scores = jnp.where(allowed, scores, masked_score)
    top_score = jnp.max(scores, -1, keepdims=True)
    expo = jnp.exp(scores - top_score)
    probs = expo / jnp.sum(expo, -1, keepdims=True)
    weights = probs.astype(jnp.bfloat16)
    output = jnp.einsum(
        "kgts,skd->tkgd", weights, all_values, preferred_element_type=jnp.float32
    ).astype(jnp.bfloat16)
    live_rows = (positions < length)[:, None, None, None]
    grad_out = jnp.where(live_rows, grad_rows, jnp.zeros((), grad_rows.dtype))
    d_vals = jnp.einsum("kgts,tkgd->skd", weights, grad_out, preferred_element_type=jnp.float32)
    d_probs = jnp.einsum("tkgd,skd->kgts", grad_out, all_values, preferred_element_type=jnp.float32)
    delta = jnp.sum(grad_out.astype(jnp.float32) * output.astype(jnp.float32), -1)
    delta = jnp.transpose(delta, (1, 2, 0))
    d_scores = (probs * (d_probs - delta[..., None])).astype(jnp.bfloat16)
    d_query = (
        jnp.einsum("kgts,skd->tkgd", d_scores, all_keys, preferred_element_type=jnp.float32) * scale
    ).astype(jnp.bfloat16)
    d_keys_all = (
        jnp.einsum("kgts,tkgd->skd", d_scores, query_rows, preferred_element_type=jnp.float32)
        * scale
    )
    prefix_grads = jnp.stack(
        [
            d_keys_all[:prefix].reshape(prefix, kv_local * head_dim),
            d_vals[:prefix].reshape(prefix, kv_local * head_dim),
        ],
        0,
    )
    return (
        output,
        d_query,
        d_keys_all[prefix:].astype(jnp.bfloat16),
        d_vals[prefix:].astype(jnp.bfloat16),
        prefix_grads,
    )


def local(queries, keys, values, prefix_keys, prefix_values, prompt_of, lengths, cotangent):
    head_q, head_k, head_v, head_g = (
        lax.all_to_all(queries, "mp", split_axis=1, concat_axis=0, tiled=True),
        lax.all_to_all(keys, "mp", split_axis=1, concat_axis=0, tiled=True),
        lax.all_to_all(values, "mp", split_axis=1, concat_axis=0, tiled=True),
        lax.all_to_all(cotangent, "mp", split_axis=1, concat_axis=0, tiled=True),
    )
    comp_count = prompt_of.shape[0]
    row_count = head_q.shape[0]
    clen = row_count // comp_count
    kv_local = head_k.shape[1] // HD
    group_size = head_q.shape[1] // head_k.shape[1]
    prefix_pair = jnp.stack([prefix_keys[0], prefix_values[0]], 0)
    received = [prefix_pair]
    for hop_count in range(1, REACH):
        received.append(shifted(prefix_pair, "dp", hop_count))
    slot_stack = jnp.stack(received, 0)
    offsets = lax.axis_index("dp") - prompt_of
    chosen = jnp.take(slot_stack, offsets, axis=0)
    query_blocks = head_q.reshape(comp_count, clen, kv_local, group_size, HD)
    grad_blocks = head_g.reshape(comp_count, clen, kv_local, group_size, HD)
    key_blocks = head_k.reshape(comp_count, clen, kv_local, HD)
    value_blocks = head_v.reshape(comp_count, clen, kv_local, HD)
    output, d_query, d_key, d_value, prefix_grads = lax.map(
        attend_block, (query_blocks, key_blocks, value_blocks, grad_blocks, chosen, lengths)
    )
    one_hot = (offsets[:, None] == jnp.arange(REACH, dtype=jnp.int32)[None, :]).astype(jnp.float32)
    slot_grads = jnp.einsum("cr,cxpf->rxpf", one_hot, prefix_grads, precision=lax.Precision.HIGHEST)
    grad_total = slot_grads[0]
    for hop_count in range(1, REACH):
        grad_total = grad_total + shifted(slot_grads[hop_count], "dp", -hop_count)
    output = output.reshape(row_count, kv_local * group_size * HD)
    d_query = d_query.reshape(row_count, kv_local * group_size * HD)
    d_key = d_key.reshape(row_count, kv_local * HD)
    d_value = d_value.reshape(row_count, kv_local * HD)
    attended, d_queries, d_keys, d_values = (
        lax.all_to_all(output, "mp", split_axis=0, concat_axis=1, tiled=True),
        lax.all_to_all(d_query, "mp", split_axis=0, concat_axis=1, tiled=True),
        lax.all_to_all(d_key, "mp", split_axis=0, concat_axis=1, tiled=True),
        lax.all_to_all(d_value, "mp", split_axis=0, concat_axis=1, tiled=True),
    )
    grad_bf = grad_total.astype(jnp.bfloat16)
    return (attended, d_queries, d_keys, d_values, grad_bf[0][None], grad_bf[1][None])


def solution(mesh):
    placed = (
        P(("dp", "mp"), None),
        P(("dp", "mp"), None),
        P(("dp", "mp"), None),
        P("dp", None, "mp"),
        P("dp", None, "mp"),
        P("dp"),
        P("dp"),
        P(("dp", "mp"), None),
    )
    return jax.shard_map(
        local,
        mesh=mesh,
        in_specs=placed,
        out_specs=(
            P(("dp", "mp"), None),
            P(("dp", "mp"), None),
            P(("dp", "mp"), None),
            P(("dp", "mp"), None),
            P("dp", None, "mp"),
            P("dp", None, "mp"),
        ),
        check_vma=False,
    )
```

profile of v0, /device:TPU:61, one launch (start us, length us, event | category | flops | bytes accessed | tf_op | source)
XLA Modules:
  0.0 483.9 jit_solution(5846359231012110896)
XLA Ops:
  2.2 8.0 %all-to-all-start = ((bf16[64,8,128]{2,0,1:T(8,128)(2,1)}), bf16[64,8,128]{2,0,1:T(8,128)(2,1)S(1)}, u32[]{:S(2)}, u32[]{:S(2)}) async-start(bf16[64,8,128]{2,0,1:T(8,128)(2,1)} %copy_bitcast_fusion.5), calls=%async_computation | async-start | bytes 262144 | tf_op jit(solution)/shard_map/all_to_all | solution.py:81
  10.2 2.0 copy.113
  12.3 4.7 all-to-all-done
  17.0 4.5 all-to-all-start.2
  21.5 1.1 constant_dynamic-update-slice_fusion.3
  22.6 5.9 %collective-permute-start.2 = (bf16[2,2048,128]{2,1,0:T(8,128)(2,1)S(1)}, bf16[2,2048,128]{2,1,0:T(8,128)(2,1)}, u32[]{:S(2)}, u32[]{:S(2)}) collective-permute-start(bf16[2,2048,128]{2,1,0:T(8,128)(2,1)S(1)} %constant_dynamic-update-slice_fusion.2), channel_id=1, source_target_pairs={{0,24},{8,32},{16,40},{24,48},{32,56},{40,64},{48,72},{56,80},{64,... | collective-permute-start | bytes 3145736 | tf_op jit(solution)/shard_map/ppermute | solution.py:16
  28.6 3.8 collective-permute-start.1
  32.4 1.9 collective-permute-start
  34.4 1.0 copy.112
  35.8 7.6 %all-to-all-start.3 = ((bf16[64,8,640]{2,0,1:T(8,128)(2,1)}), bf16[64,8,640]{2,0,1:T(8,128)(2,1)S(1)}, u32[]{:S(2)}, u32[]{:S(2)}) async-start(bf16[64,8,640]{2,0,1:T(8,128)(2,1)} %bitcast.220), calls=%async_computation.3 | async-start | bytes 1310720 | tf_op jit(solution)/shard_map/all_to_all | solution.py:82
  44.7 16.1 %collective-permute-done.2 = bf16[2,2048,128]{2,1,0:T(8,128)(2,1)} collective-permute-done((bf16[2,2048,128]{2,1,0:T(8,128)(2,1)S(1)}, bf16[2,2048,128]{2,1,0:T(8,128)(2,1)}, u32[]{:S(2)}, u32[]{:S(2)}) %collective-permute-start.2) | collective-permute-done | bytes 1048608 | tf_op jit(solution)/shard_map/ppermute | solution.py:16
  60.8 13.8 %collective-permute-done.1 = bf16[2,2048,128]{2,1,0:T(8,128)(2,1)} collective-permute-done((bf16[2,2048,128]{2,1,0:T(8,128)(2,1)S(1)}, bf16[2,2048,128]{2,1,0:T(8,128)(2,1)}, u32[]{:S(2)}, u32[]{:S(2)}) %collective-permute-start.1) | collective-permute-done | bytes 1048608 | tf_op jit(solution)/shard_map/ppermute | solution.py:16
  74.6 11.2 %collective-permute-done = bf16[2,2048,128]{2,1,0:T(8,128)(2,1)} collective-permute-done((bf16[2,2048,128]{2,1,0:T(8,128)(2,1)S(1)}, bf16[2,2048,128]{2,1,0:T(8,128)(2,1)}, u32[]{:S(2)}, u32[]{:S(2)}) %collective-permute-start) | collective-permute-done | bytes 1048608 | tf_op jit(solution)/shard_map/ppermute | solution.py:16
  85.8 3.6 pad_maximum_fusion
  89.4 4.4 gather_fusion
  93.8 6.7 %all-to-all-start.1 = ((bf16[64,8,128]{2,0,1:T(8,128)(2,1)}), bf16[64,8,128]{2,0,1:T(8,128)(2,1)S(1)}, u32[]{:S(2)}, u32[]{:S(2)}) async-start(bf16[64,8,128]{2,0,1:T(8,128)(2,1)} %copy_bitcast_fusion.4), calls=%async_computation.1 | async-start | bytes 262144 | tf_op jit(solution)/shard_map/all_to_all | solution.py:80
  100.5 1.9 broadcast_select_fusion
  102.4 1.8 reshape.228
  104.2 0.9 copy.64
  105.1 1.8 reshape.229
  106.9 1.0 copy.65
  107.9 185.7 %while.20 = (s32[]{:T(128)}, bf16[2,256,1,5,128]{1,4,3,2,0:T(8,128)(2,1)}, bf16[2,256,1,5,128]{1,4,3,2,0:T(8,128)(2,1)}, bf16[2,256,1,128]{3,1,0,2:T(8,128)(2,1)...) while((s32[]{:T(128)}, ...), condition=%wide.region_4.5_spmd, body=%wide.region_0.4_spmd.sunk | while | flops 4609578496 | bytes 193096432 | solution.py:100
  109.3 2.1 fusion.104
  112.4 3.2 fusion.105
  115.6 2.5 fusion.106
  118.1 1.8 copy-done.2
  119.9 3.7 bitcast_dynamic-update-slice_fusion.2
  125.5 7.2 %fusion.107 = bf16[1,5,256,2304]{2,3,1,0:T(8,128)(2,1)S(1)} fusion(f32[5,256]{1,0:T(8,128)S(1)} %bitcast.301, f32[5,256]{1,0:T(8,128)S(1)} %fusion.106, f32[5,256]{1,0:T(8,128)S(1)} %get-tuple-element.318, f32[2304,256,5]{1,0,2:T(8,128)} %copy-done.2, pred[256,2304]{0,1:T(8,128)(4,1)S(1)} %fusion.104, ...), kind=kOutput, calls=%fused_computation.3.clone.1 | convolution fusion | flops 776962048 | bytes 19217664 | tf_op jit(solution)/shard_map/while/body/eval_jaxpr/tkgd,skd->kgts/dot_general | solution.py:50
  132.7 1.0 fusion.108
  134.6 2.0 fusion.109
  137.4 6.2 %fusion.111 = f32[2304,1,128]{0,2,1:T(8,128)S(1)} fusion(bf16[1,256,1,5,128]{4,1,3,2,0:T(8,128)(2,1)S(1)} %constant_dynamic-slice_fusion.2, pred[256]{0:T(512)(128)(4,1)} %copy-done.22, f32[5,256]{1,0:T(8,128)S(1)} %fusion.106, f32[5,256]{1,0:T(8,128)S(1)} %get-tuple-element.318, f32[2304,256,5]{1,0,2:T(8,128)} %copy-done.2, ...), kind=kOutput, calls=%fused_computation.18.clone.1 | convolution fusion | flops 769884160 | bytes 13904128 | tf_op jit(solution)/shard_map/while/body/eval_jaxpr/kgts,tkgd->skd/dot_general | solution.py:49
  144.8 3.6 copy.121
  148.4 52.2 %dynamic_update_slice.46 = f32[2,2,2048,128]{3,0,2,1:T(2,128)} dynamic-update-slice(f32[2,2,2048,128]{3,0,2,1:T(2,128)} %get-tuple-element.343, f32[1,2,2048,128]{3,0,2,1:T(1,128)} %copy.121, s32[]{:T(128)S(6)} %copy.134, s32[]{:T(128)} %constant.83.clone.1..sunk, s32[]{:T(128)} %constant.83.clone.1..sunk, s32[]{:T(128)} %constant.83.clone.1..sunk) | dynamic-update-slice | bytes 4194308 | tf_op jit(solution)/shard_map/while/body/jit(dynamic_update_index_in_dim)/dynamic_update_slice | solution.py:100
  202.1 2.1 fusion.104
  205.2 3.2 fusion.105
  208.4 2.5 fusion.106
  210.9 1.8 copy-done.2
  212.7 3.7 bitcast_dynamic-update-slice_fusion.2
  218.2 7.2 %fusion.107 = bf16[1,5,256,2304]{2,3,1,0:T(8,128)(2,1)S(1)} fusion(f32[5,256]{1,0:T(8,128)S(1)} %bitcast.301, f32[5,256]{1,0:T(8,128)S(1)} %fusion.106, f32[5,256]{1,0:T(8,128)S(1)} %get-tuple-element.318, f32[2304,256,5]{1,0,2:T(8,128)} %copy-done.2, pred[256,2304]{0,1:T(8,128)(4,1)S(1)} %fusion.104, ...), kind=kOutput, calls=%fused_computation.3.clone.1 | convolution fusion | flops 776962048 | bytes 19217664 | tf_op jit(solution)/shard_map/while/body/eval_jaxpr/tkgd,skd->kgts/dot_general | solution.py:50
  225.5 1.0 fusion.108
  227.3 2.0 fusion.109
  230.1 6.2 %fusion.111 = f32[2304,1,128]{0,2,1:T(8,128)S(1)} fusion(bf16[1,256,1,5,128]{4,1,3,2,0:T(8,128)(2,1)S(1)} %constant_dynamic-slice_fusion.2, pred[256]{0:T(512)(128)(4,1)} %copy-done.22, f32[5,256]{1,0:T(8,128)S(1)} %fusion.106, f32[5,256]{1,0:T(8,128)S(1)} %get-tuple-element.318, f32[2304,256,5]{1,0,2:T(8,128)} %copy-done.2, ...), kind=kOutput, calls=%fused_computation.18.clone.1 | convolution fusion | flops 769884160 | bytes 13904128 | tf_op jit(solution)/shard_map/while/body/eval_jaxpr/kgts,tkgd->skd/dot_general | solution.py:49
  237.6 3.6 copy.121
  241.2 52.2 %dynamic_update_slice.46 = f32[2,2,2048,128]{3,0,2,1:T(2,128)} dynamic-update-slice(f32[2,2,2048,128]{3,0,2,1:T(2,128)} %get-tuple-element.343, f32[1,2,2048,128]{3,0,2,1:T(1,128)} %copy.121, s32[]{:T(128)S(6)} %copy.134, s32[]{:T(128)} %constant.83.clone.1..sunk, s32[]{:T(128)} %constant.83.clone.1..sunk, s32[]{:T(128)} %constant.83.clone.1..sunk) | dynamic-update-slice | bytes 4194308 | tf_op jit(solution)/shard_map/while/body/jit(dynamic_update_index_in_dim)/dynamic_update_slice | solution.py:100
  293.6 13.3 %all_to_all.140 = bf16[8,64,128]{2,1,0:T(8,128)(2,1)S(1)} all-to-all(bf16[8,64,128]{2,1,0:T(8,128)(2,1)} %bitcast.302), channel_id=1, replica_groups=mesh['dp'=32,'mp'=8] {'mp'}, dimensions={0} | all-to-all | bytes 262144 | tf_op jit(solution)/shard_map/all_to_all | solution.py:115
  306.9 4.5 all-to-all-start.7
  311.4 13.2 %fusion.68 = f32[4,2,2048,128]{3,0,2,1:T(4,128)} fusion(f32[2,2,2048,128]{3,0,2,1:T(2,128)} %get-tuple-element.386, s32[2]{0:T(128)} %copy-done.23), kind=kOutput, calls=%fused_computation.86 | convolution fusion | flops 50331656 | bytes 12582920 | tf_op jit(solution)/shard_map/cr,cxpf->rxpf/dot_general | solution.py:104
  325.4 1.6 all_to_all.116
  327.0 6.7 %all-to-all-start.4 = ((bf16[8,64,640]{2,1,0:T(8,128)(2,1)}), bf16[8,64,640]{2,1,0:T(8,128)(2,1)}, u32[]{:S(2)}, u32[]{:S(2)}) async-start(bf16[8,64,640]{2,1,0:T(8,128)(2,1)} %all_to_all.116), calls=%async_computation.4 | async-start | bytes 1310720 | tf_op jit(solution)/shard_map/all_to_all | solution.py:113
  333.7 19.8 %fusion.73 = (f32[1,2,2048,128]{3,0,2,1:T(1,128)}, f32[1,2,2048,128]{3,0,2,1:T(1,128)S(1)}, f32[1,2,2048,128]{3,0,2,1:T(1,128)}, f32[1,2,2048,128]{3,0,2,1:T(1,128)}) fusion(f32[4,2,2048,128]{3,0,2,1:T(4,128)} %fusion.68), kind=kLoop, calls=%fused_computation.93 | loop fusion | bytes 16777216 | tf_op jit(solution)/shard_map/slice | solution.py:107
  353.5 4.6 collective-permute-start.5
  358.1 2.1 collective-permute-start.4
  360.2 2.1 collective-permute-start.3
  362.4 1.6 copy.68
  364.0 1.6 all_to_all.120
  365.6 6.6 %all-to-all-start.5 = ((bf16[8,64,640]{2,1,0:T(8,128)(2,1)}), bf16[8,64,640]{2,1,0:T(8,128)(2,1)S(1)}, u32[]{:S(2)}, u32[]{:S(2)}) async-start(bf16[8,64,640]{2,1,0:T(8,128)(2,1)} %all_to_all.120), calls=%async_computation.5 | async-start | bytes 1310720 | tf_op jit(solution)/shard_map/all_to_all | solution.py:114
  373.6 2.0 copy.102
  375.6 9.7 %all-to-all-done.5 = bf16[8,64,640]{2,1,0:T(8,128)(2,1)S(1)} async-done(((bf16[8,64,640]{2,1,0:T(8,128)(2,1)}), bf16[8,64,640]{2,1,0:T(8,128)(2,1)S(1)}, u32[]{:S(2)}, u32[]{:S(2)}) %all-to-all-start.5) | async-done | bytes 655392 | tf_op jit(solution)/shard_map/all_to_all | solution.py:114
  385.3 0.9 copy.103
  386.2 17.3 %collective-permute-done.5 = f32[2,2048,128]{2,1,0:T(8,128)} collective-permute-done((f32[2,2048,128]{2,1,0:T(8,128)}, f32[2,2048,128]{2,1,0:T(8,128)}, u32[]{:S(2)}, u32[]{:S(2)}) %collective-permute-start.5) | collective-permute-done | bytes 2097184 | tf_op jit(solution)/shard_map/ppermute | solution.py:16
  403.5 52.6 %collective-permute-done.4 = f32[2,2048,128]{2,1,0:T(8,128)} collective-permute-done((f32[2,2048,128]{2,1,0:T(8,128)}, f32[2,2048,128]{2,1,0:T(8,128)}, u32[]{:S(2)}, u32[]{:S(2)}) %collective-permute-start.4) | collective-permute-done | bytes 2097184 | tf_op jit(solution)/shard_map/ppermute | solution.py:16
  456.0 23.5 %collective-permute-done.3 = f32[2,2048,128]{2,1,0:T(8,128)} collective-permute-done((f32[2,2048,128]{2,1,0:T(8,128)}, f32[2,2048,128]{2,1,0:T(8,128)}, u32[]{:S(2)}, u32[]{:S(2)}) %collective-permute-start.3) | collective-permute-done | bytes 2097184 | tf_op jit(solution)/shard_map/ppermute | solution.py:16
  479.5 3.3 add_convert_fusion
  482.8 1.0 fusion.74
  (139 shorter events, 19.4 us)
Async XLA Ops:
  0.6 0.9 copy-start
  0.7 21.9 %copy-start.18 = (bf16[1,2048,128]{2,1,0:T(8,128)(2,1)S(1)}, bf16[1,2048,128]{2,1,0:T(8,128)(2,1)}, u32[]{:S(2)}) copy-start(bf16[1,2048,128]{2,1,0:T(8,128)(2,1)} %param.14) | copy-start | bytes 1572868
  0.7 33.7 %copy-start.12 = (bf16[64,5120]{1,0:T(8,128)(2,1)S(1)}, bf16[64,5120]{1,0:T(8,128)(2,1)}, u32[]{:S(2)}) copy-start(bf16[64,5120]{1,0:T(8,128)(2,1)} %param.17) | copy-start | bytes 1966084
  0.7 42.7 %copy-start.24 = (s32[2]{0:T(128)S(1)}, s32[2]{0:T(128)}, u32[]{:S(2)}) copy-start(s32[2]{0:T(128)} %param.15) | copy-start | bytes 28
  0.7 43.3 %copy-start.19 = (bf16[64,1024]{1,0:T(8,128)(2,1)S(1)}, bf16[64,1024]{1,0:T(8,128)(2,1)}, u32[]{:S(2)}) copy-start(bf16[64,1024]{1,0:T(8,128)(2,1)} %param.11) | copy-start | bytes 393220
  2.2 14.8 %all-to-all-start = ((bf16[64,8,128]{2,0,1:T(8,128)(2,1)}), bf16[64,8,128]{2,0,1:T(8,128)(2,1)S(1)}, u32[]{:S(2)}, u32[]{:S(2)}) async-start(bf16[64,8,128]{2,0,1:T(8,128)(2,1)} %copy_bitcast_fusion.5), calls=%async_computation | async-start | bytes 262144 | tf_op jit(solution)/shard_map/all_to_all | solution.py:81
  17.0 18.8 %all-to-all-start.2 = ((bf16[64,8,640]{2,0,1:T(8,128)(2,1)}), bf16[64,8,640]{2,0,1:T(8,128)(2,1)S(1)}, u32[]{:S(2)}, u32[]{:S(2)}) async-start(bf16[64,8,640]{2,0,1:T(8,128)(2,1)} %bitcast.221), calls=%async_computation.2 | async-start | bytes 1310720 | tf_op jit(solution)/shard_map/all_to_all | solution.py:79
  22.6 38.2 %collective-permute-start.2 = (bf16[2,2048,128]{2,1,0:T(8,128)(2,1)S(1)}, bf16[2,2048,128]{2,1,0:T(8,128)(2,1)}, u32[]{:S(2)}, u32[]{:S(2)}) collective-permute-start(bf16[2,2048,128]{2,1,0:T(8,128)(2,1)S(1)} %constant_dynamic-update-slice_fusion.2), channel_id=1, source_target_pairs={{0,24},{8,32},{16,40},{24,48},{32,56},{40,64},{48,72},{56,80},{64,... | collective-permute-start | bytes 3145736 | tf_op jit(solution)/shard_map/ppermute | solution.py:16
  28.6 46.0 %collective-permute-start.1 = (bf16[2,2048,128]{2,1,0:T(8,128)(2,1)S(1)}, bf16[2,2048,128]{2,1,0:T(8,128)(2,1)}, u32[]{:S(2)}, u32[]{:S(2)}) collective-permute-start(bf16[2,2048,128]{2,1,0:T(8,128)(2,1)S(1)} %constant_dynamic-update-slice_fusion.2), channel_id=1, source_target_pairs={{0,16},{8,24},{16,32},{24,40},{32,48},{40,56},{48,64},{56,72},{64,... | collective-permute-start | bytes 3145736 | tf_op jit(solution)/shard_map/ppermute | solution.py:16
  32.4 53.4 %collective-permute-start = (bf16[2,2048,128]{2,1,0:T(8,128)(2,1)S(1)}, bf16[2,2048,128]{2,1,0:T(8,128)(2,1)}, u32[]{:S(2)}, u32[]{:S(2)}) collective-permute-start(bf16[2,2048,128]{2,1,0:T(8,128)(2,1)S(1)} %constant_dynamic-update-slice_fusion.2), channel_id=1, source_target_pairs={{0,8},{8,16},{16,24},{24,32},{32,40},{40,48},{48,56},{56,64},{64,7... | collective-permute-start | bytes 3145736 | tf_op jit(solution)/shard_map/ppermute | solution.py:16
  35.8 53.7 %copy-start.8 = (bf16[64,8,640]{2,0,1:T(8,128)(2,1)}, bf16[64,8,640]{2,0,1:T(8,128)(2,1)S(1)}, u32[]{:S(2)}) copy-start(bf16[64,8,640]{2,0,1:T(8,128)(2,1)S(1)} %all-to-all-done.2) | copy-start | bytes 1966084
  35.8 58.0 %all-to-all-start.3 = ((bf16[64,8,640]{2,0,1:T(8,128)(2,1)}), bf16[64,8,640]{2,0,1:T(8,128)(2,1)S(1)}, u32[]{:S(2)}, u32[]{:S(2)}) async-start(bf16[64,8,640]{2,0,1:T(8,128)(2,1)} %bitcast.220), calls=%async_computation.3 | async-start | bytes 1310720 | tf_op jit(solution)/shard_map/all_to_all | solution.py:82
  43.4 0.6 copy-start.23
  93.8 6.7 %copy-start.9 = (bf16[64,8,640]{2,0,1:T(8,128)(2,1)}, bf16[64,8,640]{2,0,1:T(8,128)(2,1)S(1)}, u32[]{:S(2)}) copy-start(bf16[64,8,640]{2,0,1:T(8,128)(2,1)S(1)} %all-to-all-done.3) | copy-start | bytes 1966084
  93.8 14.1 %all-to-all-start.1 = ((bf16[64,8,128]{2,0,1:T(8,128)(2,1)}), bf16[64,8,128]{2,0,1:T(8,128)(2,1)S(1)}, u32[]{:S(2)}, u32[]{:S(2)}) async-start(bf16[64,8,128]{2,0,1:T(8,128)(2,1)} %copy_bitcast_fusion.4), calls=%async_computation.1 | async-start | bytes 262144 | tf_op jit(solution)/shard_map/all_to_all | solution.py:80
  102.4 5.5 %copy-start.25 = (s32[2]{0:T(128)S(1)}, s32[2]{0:T(128)}, u32[]{:S(2)}) copy-start(s32[2]{0:T(128)} %param.16) | copy-start | bytes 28
  107.9 3.5 copy-start.10
  107.9 7.7 %copy-start.3 = (bf16[2,2,2048,128]{3,2,1,0:T(8,128)(2,1)}, bf16[2,2,2048,128]{3,2,1,0:T(8,128)(2,1)S(1)}, u32[]{:S(2)}) copy-start(bf16[2,2,2048,128]{3,2,1,0:T(8,128)(2,1)S(1)} %get-tuple-element.359) | copy-start | bytes 6291460 | tf_op jit(solution)/shard_map/while
  112.4 5.7 %copy-start.5 = (bf16[2048,1,128]{2,0,1:T(8,128)(2,1)}, bf16[2048,1,128]{2,0,1:T(8,128)(2,1)S(1)}, u32[]{:S(2)}) copy-start(bf16[2048,1,128]{2,0,1:T(8,128)(2,1)S(1)} %get-tuple-element.320) | copy-start | bytes 1572868 | tf_op jit(solution)/shard_map/while
  115.6 4.3 copy-start.2
  115.6 4.3 copy-start.13
  119.9 4.5 copy-start.6
  123.6 0.8 copy-start.14
  125.3 7.3 %copy-start.22 = (pred[256]{0:T(512)(128)(4,1)}, pred[256]{0:T(512)(128)(4,1)S(1)}, u32[]{:S(2)}) copy-start(pred[256]{0:T(512)(128)(4,1)S(1)} %iota_compare_fusion.3) | copy-start | bytes 772 | tf_op jit(solution)/shard_map/while
  125.5 7.2 %copy-start.16 = (bf16[2,256,1,5,128]{1,4,3,2,0:T(8,128)(2,1)S(1)}, bf16[2,256,1,5,128]{1,4,3,2,0:T(8,128)(2,1)}, u32[]{:S(2)}) copy-start(bf16[2,256,1,5,128]{1,4,3,2,0:T(8,128)(2,1)} %get-tuple-element.340) | copy-start | bytes 1966084 | tf_op jit(solution)/shard_map/while
  132.7 1.9 copy-start.7
  133.7 0.8 copy-start.17
  134.5 2.1 copy-start.20
  136.7 0.7 copy-start.21
  144.8 55.8 %copy-start.11 = (bf16[2,256,1,128]{3,1,2,0:T(8,128)(2,1)S(1)}, bf16[2,256,1,128]{3,1,2,0:T(8,128)(2,1)}, u32[]{:S(2)}) copy-start(bf16[2,256,1,128]{3,1,2,0:T(8,128)(2,1)} %copy-done.10) | copy-start | bytes 393220 | tf_op jit(solution)/shard_map/while
  144.8 55.8 %copy-start.26 = (s32[2]{0:T(128)S(1)}, s32[2]{0:T(128)}, u32[]{:S(2)}) copy-start(s32[2]{0:T(128)} %get-tuple-element.396) | copy-start | bytes 28 | tf_op jit(solution)/shard_map/while
  148.4 52.2 %copy-start.4 = (bf16[2,2,2048,128]{3,2,1,0:T(8,128)(2,1)S(1)}, bf16[2,2,2048,128]{3,2,1,0:T(8,128)(2,1)}, u32[]{:S(2)}) copy-start(bf16[2,2,2048,128]{3,2,1,0:T(8,128)(2,1)} %copy-done.3) | copy-start | bytes 6291460 | tf_op jit(solution)/shard_map/while
  200.6 3.6 copy-start.10
  200.6 7.7 %copy-start.3 = (bf16[2,2,2048,128]{3,2,1,0:T(8,128)(2,1)}, bf16[2,2,2048,128]{3,2,1,0:T(8,128)(2,1)S(1)}, u32[]{:S(2)}) copy-start(bf16[2,2,2048,128]{3,2,1,0:T(8,128)(2,1)S(1)} %get-tuple-element.359) | copy-start | bytes 6291460 | tf_op jit(solution)/shard_map/while
  205.1 5.7 %copy-start.5 = (bf16[2048,1,128]{2,0,1:T(8,128)(2,1)}, bf16[2048,1,128]{2,0,1:T(8,128)(2,1)S(1)}, u32[]{:S(2)}) copy-start(bf16[2048,1,128]{2,0,1:T(8,128)(2,1)S(1)} %get-tuple-element.320) | copy-start | bytes 1572868 | tf_op jit(solution)/shard_map/while
  208.3 4.3 copy-start.2
  208.4 4.3 copy-start.13
  212.7 4.5 copy-start.6
  216.4 0.8 copy-start.14
  218.1 7.3 %copy-start.22 = (pred[256]{0:T(512)(128)(4,1)}, pred[256]{0:T(512)(128)(4,1)S(1)}, u32[]{:S(2)}) copy-start(pred[256]{0:T(512)(128)(4,1)S(1)} %iota_compare_fusion.3) | copy-start | bytes 772 | tf_op jit(solution)/shard_map/while
  218.2 7.2 %copy-start.16 = (bf16[2,256,1,5,128]{1,4,3,2,0:T(8,128)(2,1)S(1)}, bf16[2,256,1,5,128]{1,4,3,2,0:T(8,128)(2,1)}, u32[]{:S(2)}) copy-start(bf16[2,256,1,5,128]{1,4,3,2,0:T(8,128)(2,1)} %get-tuple-element.340) | copy-start | bytes 1966084 | tf_op jit(solution)/shard_map/while
  225.4 1.9 copy-start.7
  226.5 0.8 copy-start.17
  227.3 2.1 copy-start.20
  229.5 0.7 copy-start.21
  237.5 55.8 %copy-start.11 = (bf16[2,256,1,128]{3,1,2,0:T(8,128)(2,1)S(1)}, bf16[2,256,1,128]{3,1,2,0:T(8,128)(2,1)}, u32[]{:S(2)}) copy-start(bf16[2,256,1,128]{3,1,2,0:T(8,128)(2,1)} %copy-done.10) | copy-start | bytes 393220 | tf_op jit(solution)/shard_map/while
  237.5 55.8 %copy-start.26 = (s32[2]{0:T(128)S(1)}, s32[2]{0:T(128)}, u32[]{:S(2)}) copy-start(s32[2]{0:T(128)} %get-tuple-element.396) | copy-start | bytes 28 | tf_op jit(solution)/shard_map/while
  241.2 52.2 %copy-start.4 = (bf16[2,2,2048,128]{3,2,1,0:T(8,128)(2,1)S(1)}, bf16[2,2,2048,128]{3,2,1,0:T(8,128)(2,1)}, u32[]{:S(2)}) copy-start(bf16[2,2,2048,128]{3,2,1,0:T(8,128)(2,1)} %copy-done.3) | copy-start | bytes 6291460 | tf_op jit(solution)/shard_map/while
  306.9 20.1 %all-to-all-start.7 = ((bf16[8,64,128]{2,1,0:T(8,128)(2,1)}), bf16[8,64,128]{2,1,0:T(8,128)(2,1)S(1)}, u32[]{:S(2)}, u32[]{:S(2)}) async-start(bf16[8,64,128]{2,1,0:T(8,128)(2,1)} %bitcast.303), calls=%async_computation.7 | async-start | bytes 262144 | tf_op jit(solution)/shard_map/all_to_all | solution.py:116
  311.4 13.2 %copy-start.15 = (bf16[2,256,1,5,128]{1,4,3,2,0:T(8,128)(2,1)S(1)}, bf16[2,256,1,5,128]{1,4,3,2,0:T(8,128)(2,1)}, u32[]{:S(2)}) copy-start(bf16[2,256,1,5,128]{1,4,3,2,0:T(8,128)(2,1)} %get-tuple-element.382) | copy-start | bytes 1966084
  327.0 38.6 %all-to-all-start.4 = ((bf16[8,64,640]{2,1,0:T(8,128)(2,1)}), bf16[8,64,640]{2,1,0:T(8,128)(2,1)}, u32[]{:S(2)}, u32[]{:S(2)}) async-start(bf16[8,64,640]{2,1,0:T(8,128)(2,1)} %all_to_all.116), calls=%async_computation.4 | async-start | bytes 1310720 | tf_op jit(solution)/shard_map/all_to_all | solution.py:113
  353.5 50.0 %collective-permute-start.5 = (f32[2,2048,128]{2,1,0:T(8,128)}, f32[2,2048,128]{2,1,0:T(8,128)}, u32[]{:S(2)}, u32[]{:S(2)}) collective-permute-start(f32[2,2048,128]{2,1,0:T(8,128)} %bitcast.65), channel_id=1, source_target_pairs={{24,0},{32,8},{40,16},{48,24},{56,32},{64,40},{72,48},{80,56},{88,... | collective-permute-start | bytes 6291464 | tf_op jit(solution)/shard_map/ppermute | solution.py:16
  358.1 97.9 %collective-permute-start.4 = (f32[2,2048,128]{2,1,0:T(8,128)}, f32[2,2048,128]{2,1,0:T(8,128)}, u32[]{:S(2)}, u32[]{:S(2)}) collective-permute-start(f32[2,2048,128]{2,1,0:T(8,128)} %bitcast.64), channel_id=1, source_target_pairs={{16,0},{24,8},{32,16},{40,24},{48,32},{56,40},{64,48},{72,56},{80,... | collective-permute-start | bytes 6291464 | tf_op jit(solution)/shard_map/ppermute | solution.py:16
  360.2 119.3 %collective-permute-start.3 = (f32[2,2048,128]{2,1,0:T(8,128)}, f32[2,2048,128]{2,1,0:T(8,128)}, u32[]{:S(2)}, u32[]{:S(2)}) collective-permute-start(f32[2,2048,128]{2,1,0:T(8,128)} %bitcast.63), channel_id=1, source_target_pairs={{8,0},{16,8},{24,16},{32,24},{40,32},{48,40},{56,48},{64,56},{72,6... | collective-permute-start | bytes 6291464 | tf_op jit(solution)/shard_map/ppermute | solution.py:16
  365.6 19.7 %all-to-all-start.5 = ((bf16[8,64,640]{2,1,0:T(8,128)(2,1)}), bf16[8,64,640]{2,1,0:T(8,128)(2,1)S(1)}, u32[]{:S(2)}, u32[]{:S(2)}) async-start(bf16[8,64,640]{2,1,0:T(8,128)(2,1)} %all_to_all.120), calls=%async_computation.5 | async-start | bytes 1310720 | tf_op jit(solution)/shard_map/all_to_all | solution.py:114
  479.5 4.3 copy-start.1
where the time goes:
time: 492 us; the launch traced here: 484 us
  local copies, waits for them, and re-layouts  173 us (35%)
  waiting for transfers between devices  149 us (30%)
  starting transfers between devices  65.1 us (13%)
  matrix products  59.7 us (12%)
  other arithmetic  21.2 us (4%)
  blocking collectives  13.3 us (3%)
    ppermute x6, waiting for transfers between devices, shifted(): return lax.ppermute(shard, axis, pairs)  134 us
    dynamic_update_slice x12, local copies, waits for them, and re-layouts, local(): lax.map(attend_block, (query_blocks, key_blocks, value_blocks, grad_block...  113 us
    ppermute x6, starting transfers between devices, shifted(): return lax.ppermute(shard, axis, pairs)  20.5 us
    slice x1, local copies, waits for them, and re-layouts, local(): grad_total = grad_total + shifted(slot_grads[hop_count], 'dp', -hop_count)  19.8 us
    dot_general x2, matrix products, attend_block(): jnp.einsum('tkgd,skd->kgts', grad_out, all_values, preferred_element_type...  14.4 us
    all_to_all x1, blocking collectives, local(): lax.all_to_all(d_key, 'mp', split_axis=0, concat_axis=1, tiled=True)  13.3 us
    dot_general x1, matrix products, local(): jnp.einsum('cr,cxpf->rxpf', one_hot, prefix_grads, precision=lax.Precisio...  13.2 us
    dot_general x2, matrix products, attend_block(): jnp.einsum('kgts,tkgd->skd', weights, grad_out, preferred_element_type=jn...  12.3 us
  transfers between devices with their start and end apart: 13, of which 9 were waited for; matrix products, arithmetic and copies ran while one was open for 12% of the time, Pallas kernels for 0%

commit v1 on v0

v1 whole, which is shorter than its diff:
```python
import jax
import jax.numpy as jnp
from jax import lax
from jax.experimental import pallas as pl
from jax.experimental.pallas import tpu as pltpu
from jax.sharding import PartitionSpec as P

HD = 128
GROUP = 5
REACH = 4
CLEN = 256
PREFIX = 2048
CHUNK = 256
STEPS = PREFIX // CHUNK + 1
KEYS = PREFIX + CLEN
SCALE = HD**-0.5
SCALE_LOG2E = SCALE * 1.4426950408889634
MASKED = -1e30
HEADS_A = 2
HEADS_B = GROUP - HEADS_A
F32 = jnp.float32
BF16 = jnp.bfloat16


def nt(a, b):
    return lax.dot_general(a, b, (((1,), (1,)), ((), ())), preferred_element_type=F32)


def nn(a, b):
    return lax.dot_general(a, b, (((1,), (0,)), ((), ())), preferred_element_type=F32)


def pack_kernel(q_ref, k_ref, v_ref, g_ref, a_ref, b_ref):
    cut = HEADS_A * HD
    a_ref[0, :, :cut] = q_ref[:, :cut]
    a_ref[0, :, cut : 2 * cut] = g_ref[:, :cut]
    a_ref[0, :, 2 * cut : 2 * cut + HD] = k_ref[...]
    a_ref[0, :, 2 * cut + HD :] = v_ref[...]
    rest = HEADS_B * HD
    b_ref[0, :, :rest] = q_ref[:, cut:]
    b_ref[0, :, rest:] = g_ref[:, cut:]


def pack(queries, keys, values, cotangent, parts):
    rows = queries.shape[0]
    wide = pl.BlockSpec((rows, GROUP * HD), lambda m: (0, m))
    thin = pl.BlockSpec((rows, HD), lambda m: (0, m))
    wa, wb = (2 * HEADS_A + 2) * HD, 2 * HEADS_B * HD
    return pl.pallas_call(
        pack_kernel,
        grid=(parts,),
        in_specs=[wide, thin, thin, wide],
        out_specs=[
            pl.BlockSpec((1, rows, wa), lambda m: (m, 0, 0)),
            pl.BlockSpec((1, rows, wb), lambda m: (m, 0, 0)),
        ],
        out_shape=[
            jax.ShapeDtypeStruct((parts, rows, wa), BF16),
            jax.ShapeDtypeStruct((parts, rows, wb), BF16),
        ],
        name="pack",
    )(queries, keys, values, cotangent)


def unpack_kernel(a_ref, b_ref, o_ref, dq_ref, dk_ref, dv_ref):
    cut = HEADS_A * HD
    o_ref[:, :cut] = a_ref[0, :, :cut]
    dq_ref[:, :cut] = a_ref[0, :, cut:]
    rest = HEADS_B * HD
    o_ref[:, cut:] = b_ref[0, :, :rest]
    dq_ref[:, cut:] = b_ref[0, :, rest : 2 * rest]
    dk_ref[...] = b_ref[0, :, 2 * rest : 2 * rest + HD]
    dv_ref[...] = b_ref[0, :, 2 * rest + HD :]


def unpack(out_a, out_b):
    parts, rows, wa = out_a.shape
    wb = out_b.shape[2]
    wide = pl.BlockSpec((rows, GROUP * HD), lambda m: (0, m))
    thin = pl.BlockSpec((rows, HD), lambda m: (0, m))
    return pl.pallas_call(
        unpack_kernel,
        grid=(parts,),
        in_specs=[
            pl.BlockSpec((1, rows, wa), lambda m: (m, 0, 0)),
            pl.BlockSpec((1, rows, wb), lambda m: (m, 0, 0)),
        ],
        out_specs=[wide, wide, thin, thin],
        out_shape=[
            jax.ShapeDtypeStruct((rows, parts * GROUP * HD), BF16),
            jax.ShapeDtypeStruct((rows, parts * GROUP * HD), BF16),
            jax.ShapeDtypeStruct((rows, parts * HD), BF16),
            jax.ShapeDtypeStruct((rows, parts * HD), BF16),
        ],
        name="unpack",
    )(out_a, out_b)


def attend_kernel(heads, first, last, with_prev, *refs):
    slot_ref, len_ref, q_ref, g_ref, k_ref, v_ref, pk_ref, pv_ref = refs[:8]
    refs = refs[8:]
    if not first:
        acc_in_ref, refs = refs[0], refs[1:]
    if with_prev:
        refs = refs[1:]
    out_ref, acc_ref, s_ref, w_ref, kt_ref, vt_ref = refs
    j = pl.program_id(0)
    length = len_ref[slot_ref[0]]

    def key_rows(i):
        return k_ref[...] if i == STEPS - 1 else pk_ref[i * CHUNK : (i + 1) * CHUNK, :]

    def value_rows(i):
        return v_ref[...] if i == STEPS - 1 else pv_ref[i * CHUNK : (i + 1) * CHUNK, :]

    @pl.when(j == 0)
    def _():
        for i in range(STEPS):
            kt_ref[:, i * CHUNK : (i + 1) * CHUNK] = key_rows(i).T
            vt_ref[:, i * CHUNK : (i + 1) * CHUNK] = value_rows(i).T
        if first:
            acc_ref[...] = jnp.zeros_like(acc_ref)
        else:
            acc_ref[...] = acc_in_ref[...]

    q = q_ref[...]
    row = lax.broadcasted_iota(jnp.int32, (CLEN, HD), 0)
    g = jnp.where(row < length, g_ref[...], jnp.zeros((), BF16))
    gt = g.T
    top = jnp.full((1, CLEN), MASKED, F32)
    for i in range(STEPS):
        s = nt(key_rows(i), q)
        if i == STEPS - 1:
            kp = lax.broadcasted_iota(jnp.int32, (CHUNK, CLEN), 0)
            qp = lax.broadcasted_iota(jnp.int32, (CHUNK, CLEN), 1)
            s = jnp.where((kp <= qp) & (kp < length), s, MASKED)
        s_ref[i * CHUNK : (i + 1) * CHUNK, :] = s
        top = jnp.maximum(top, jnp.max(s, 0, keepdims=True))
    total = jnp.zeros((1, CLEN), F32)
    for i in range(STEPS):
        e = jnp.exp2((s_ref[i * CHUNK : (i + 1) * CHUNK, :] - top) * SCALE_LOG2E)
        total = total + jnp.sum(e, 0, keepdims=True)
        s_ref[i * CHUNK : (i + 1) * CHUNK, :] = e
    inv = 1.0 / total
    ot = jnp.zeros((HD, CLEN), F32)
    for i in range(STEPS):
        p = s_ref[i * CHUNK : (i + 1) * CHUNK, :] * inv
        w = p.astype(BF16)
        s_ref[i * CHUNK : (i + 1) * CHUNK, :] = p
        w_ref[i * CHUNK : (i + 1) * CHUNK, :] = w
        ot = ot + nn(vt_ref[:, i * CHUNK : (i + 1) * CHUNK], w)
    ob = ot.astype(BF16)
    out_ref[:, pl.ds(pl.multiple_of(j * HD, HD), HD)] = ob.T
    delta = jnp.sum(gt.astype(F32) * ob.astype(F32), 0, keepdims=True)
    dqt = jnp.zeros((HD, CLEN), F32)
    for i in range(STEPS):
        rows = slice(i * CHUNK, (i + 1) * CHUNK)
        dp = nt(value_rows(i), g)
        ds = (s_ref[rows, :] * (dp - delta)).astype(BF16)
        acc_ref[1, rows, :] += nn(w_ref[rows, :], g)
        acc_ref[0, rows, :] += nn(ds, q)
        dqt = dqt + nn(kt_ref[:, rows], ds)
    out_ref[:, pl.ds(pl.multiple_of((heads + j) * HD, HD), HD)] = (dqt * SCALE).astype(BF16).T
    if last:

        @pl.when(j == heads - 1)
        def _():
            acc_ref[0] = acc_ref[0] * SCALE
            out_ref[:, 2 * heads * HD : (2 * heads + 1) * HD] = acc_ref[0, PREFIX:, :].astype(BF16)
            out_ref[:, (2 * heads + 1) * HD :] = acc_ref[1, PREFIX:, :].astype(BF16)


def attend(heads, first, last, slot, lengths, rows_in, kv_rows, kv_col, prefix, acc, prev, name):
    rows = rows_in.shape[0]
    width = (2 * heads + (2 if last else 0)) * HD
    in_specs = [
        pl.BlockSpec((CLEN, HD), lambda j, s, n: (s[0], j)),
        pl.BlockSpec((CLEN, HD), lambda j, s, n: (s[0], heads + j)),
        pl.BlockSpec((CLEN, HD), lambda j, s, n: (s[0], kv_col)),
        pl.BlockSpec((CLEN, HD), lambda j, s, n: (s[0], kv_col + 1)),
        pl.BlockSpec((PREFIX, HD), lambda j, s, n: (0, 0)),
        pl.BlockSpec((PREFIX, HD), lambda j, s, n: (0, 0)),
    ]
    args = [rows_in, rows_in, kv_rows, kv_rows, *prefix]
    aliases = {}
    acc_spec = pl.BlockSpec((2, KEYS, HD), lambda j, s, n: (0, 0, 0))
    if not first:
        in_specs.append(acc_spec)
        args.append(acc)
    if prev is not None:
        aliases[2 + len(args)] = 0
        in_specs.append(pl.BlockSpec(memory_space=pl.ANY))
        args.append(prev)
    return pl.pallas_call(
        lambda *refs: attend_kernel(heads, first, last, prev is not None, *refs),
        grid_spec=pltpu.PrefetchScalarGridSpec(
            num_scalar_prefetch=2,
            grid=(heads,),
            in_specs=in_specs,
            out_specs=[pl.BlockSpec((CLEN, width), lambda j, s, n: (s[0], 0)), acc_spec],
            scratch_shapes=[
                pltpu.VMEM((KEYS, CLEN), F32),
                pltpu.VMEM((KEYS, CLEN), BF16),
                pltpu.VMEM((HD, KEYS), BF16),
                pltpu.VMEM((HD, KEYS), BF16),
            ],
        ),
        out_shape=[
            jax.ShapeDtypeStruct((rows, width), BF16),
            jax.ShapeDtypeStruct((2, KEYS, HD), F32),
        ],
        input_output_aliases=aliases,
        compiler_params=pltpu.CompilerParams(vmem_limit_bytes=40 * 1024 * 1024),
        cost_estimate=pl.CostEstimate(
            flops=heads * 12 * KEYS * CLEN * HD * 2, bytes_accessed=8 << 20, transcendentals=0
        ),
        name=name,
    )(slot, lengths, *args)


def exchange(rows, parts):
    out = lax.all_to_all(rows, "mp", split_axis=0, concat_axis=0, tiled=True)
    return out


def local(queries, keys, values, prefix_keys, prefix_values, prompt_of, lengths, cotangent):
    parts = lax.axis_size("mp")
    groups = lax.axis_size("dp") // REACH
    me = lax.axis_index("dp")
    leader = me % REACH == 0
    own = jnp.where(prompt_of[0] == me, 0, 1).astype(jnp.int32)
    own_slot = own[None]
    lead_slot = 1 - own_slot
    pk, pv = prefix_keys[0], prefix_values[0]

    def send(x, pairs):
        return lax.ppermute(
            x, "dp", [(REACH * n + a, REACH * n + b) for n in range(groups) for a, b in pairs]
        )

    far_k = send(pk, [(0, 2)])
    far_v = send(pv, [(0, 2)])
    base_k = jnp.where(leader, pk, far_k)
    base_v = jnp.where(leader, pv, far_v)
    near_k = send(base_k, [(0, 1), (2, 3)])
    near_v = send(base_v, [(0, 1), (2, 3)])
    odd = me % 2 == 1
    lead_k = jnp.where(odd, near_k, base_k)
    lead_v = jnp.where(odd, near_v, base_v)

    send_a, send_b = pack(queries, keys, values, cotangent, parts)
    rows_a = exchange(send_a, parts).reshape(-1, send_a.shape[2])
    rows_b = exchange(send_b, parts).reshape(-1, send_b.shape[2])
    kv = 2 * HEADS_A
    out_a, acc_own = attend(
        HEADS_A, True, False, own_slot, lengths, rows_a, rows_a, kv, (pk, pv), None, None, "own_a"
    )
    out_a, acc_lead = attend(
        HEADS_A, True, False, lead_slot, lengths, rows_a, rows_a, kv, (lead_k, lead_v), None, out_a, "lead_a"
    )
    out_b, acc_lead = attend(
        HEADS_B, False, True, lead_slot, lengths, rows_b, rows_a, kv, (lead_k, lead_v), acc_lead, None, "lead_b"
    )
    out_b, acc_own = attend(
        HEADS_B, False, True, own_slot, lengths, rows_b, rows_a, kv, (pk, pv), acc_own, out_b, "own_b"
    )
    rows = queries.shape[0]
    back_a = exchange(out_a.reshape(parts, rows, -1), parts)
    back_b = exchange(out_b.reshape(parts, rows, -1), parts)

    lead_grads = acc_lead[:, :PREFIX]
    near = send(lead_grads, [(1, 0), (3, 2)])
    pair_sum = lead_grads + near
    far = send(pair_sum, [(2, 0)])
    grads = acc_own[:, :PREFIX] + jnp.where(leader, pair_sum + far, 0.0)
    grads = grads.astype(BF16)
    attended, d_queries, d_keys, d_values = unpack(back_a, back_b)
    return (attended, d_queries, d_keys, d_values, grads[0][None], grads[1][None])


def solution(mesh):
    rows = P(("dp", "mp"), None)
    heads = P("dp", None, "mp")
    return jax.shard_map(
        local,
        mesh=mesh,
        in_specs=(rows, rows, rows, heads, heads, P("dp"), P("dp"), rows),
        out_specs=(rows, rows, rows, rows, heads, heads),
        check_vma=False,
    )
```

time: 492 us -> 155 us (0.32)
  the two profiles are of different devices: /device:TPU:61 before, /device:TPU:13 now
where the time goes in v1:
time: 155 us; the launch traced here: 154 us
  Pallas kernels  46.9 us (30%)
  blocking collectives  35.4 us (23%)
  starting transfers between devices  26.8 us (17%)
  waiting for transfers between devices  20.4 us (13%)
  local copies, waits for them, and re-layouts  13.2 us (9%)
  other arithmetic  10.2 us (7%)
    pallas_call x4, Pallas kernels, attend(): pl.pallas_call(lambda *refs: attend_kernel(heads, first, last, prev is no...  35.9 us
    all_to_all x1, blocking collectives, exchange(): out = lax.all_to_all(rows, 'mp', split_axis=0, concat_axis=0, tiled=True)  35.4 us
    all_to_all x3, waiting for transfers between devices, exchange(): out = lax.all_to_all(rows, 'mp', split_axis=0, concat_axis=0, tiled=True)  20.4 us
    all_to_all x3, starting transfers between devices, exchange(): out = lax.all_to_all(rows, 'mp', split_axis=0, concat_axis=0, tiled=True)  16.1 us
    unnamed x42, local copies, waits for them, and re-layouts  10.7 us
    ppermute x6, starting transfers between devices, send(): lax.ppermute(x, 'dp', [(REACH * n + a, REACH * n + b) for n in range(grou...  10.7 us
    pallas_call x1, Pallas kernels, pack(): pl.pallas_call(pack_kernel, grid=(parts,), in_specs=[wide, thin, thin, wi...  5.61 us
    pallas_call x1, Pallas kernels, unpack(): pl.pallas_call(unpack_kernel, grid=(parts,), in_specs=[pl.BlockSpec((1, r...  5.47 us
  transfers between devices with their start and end apart: 9, of which 3 were waited for; matrix products, arithmetic and copies ran while one was open for 5% of the time, Pallas kernels for 24%

profile of v1, /device:TPU:13, one launch (start us, length us, event | category | flops | bytes accessed | tf_op | source)
XLA Modules:
  0.0 153.9 jit_solution(1592775753514914271)
XLA Ops:
  0.6 0.0 copy-start.6
  0.6 0.0 copy-start.8
  0.7 0.8 collective-permute-start
  1.5 5.6 %pack.1 = (bf16[8,64,768]{2,1,0:T(8,128)(2,1)}, bf16[8,64,768]{2,1,0:T(8,128)(2,1)}) custom-call(bf16[64,5120]{1,0:T(8,128)(2,1)} %q_ref.1, bf16[64,1024]{1,0:T(8,128)(2,1)} %k_ref.1, bf16[64,1024]{1,0:T(8,128)(2,1)} %v_ref.1, bf16[64,5120]{1,0:T(8,128)(2,1)} %g_ref.1), custom_call_target="tpu_custom_call" | custom-call | tf_op jit(solution)/shard_map/pack/pallas_call | solution.py:49
  7.1 8.3 %all-to-all-start = ((bf16[8,64,768]{2,1,0:T(8,128)(2,1)}), bf16[8,64,768]{2,1,0:T(8,128)(2,1)S(1)}, u32[]{:S(2)}, u32[]{:S(2)}) async-start(bf16[8,64,768]{2,1,0:T(8,128)(2,1)} %get-tuple-element.20), calls=%async_computation | async-start | bytes 1572864 | tf_op jit(solution)/shard_map/all_to_all | solution.py:222
  15.4 0.0 copy-done.8
  15.4 1.5 collective-permute-start.2
  16.9 0.0 collective-permute-done
  16.9 0.0 copy-done.6
  16.9 0.1 broadcast_select_fusion.1
  17.0 1.3 collective-permute-start.1
  18.3 0.0 collective-permute-done.2
  18.3 1.9 %broadcast_select_fusion = bf16[2048,128]{1,0:T(8,128)(2,1)} fusion(bf16[2048,128]{1,0:T(8,128)(2,1)} %collective-permute-done.2, pred[]{:T(512)S(6)} %eq.14, bf16[1,2048,128]{2,1,0:T(8,128)(2,1)S(1)} %copy-done.8), kind=kLoop, calls=%fused_computation.1 | loop fusion | flops 262144 | bytes 1572865 | tf_op jit(solution)/shard_map/jit(_where)/select_n | solution.py:244
  20.2 1.3 collective-permute-start.3
  21.5 0.0 copy-done.20
  21.5 17.5 %all-to-all-done = bf16[8,64,768]{2,1,0:T(8,128)(2,1)S(1)} async-done(((bf16[8,64,768]{2,1,0:T(8,128)(2,1)}), bf16[8,64,768]{2,1,0:T(8,128)(2,1)S(1)}, u32[]{:S(2)}, u32[]{:S(2)}) %all-to-all-start) | async-done | bytes 786464 | tf_op jit(solution)/shard_map/all_to_all | solution.py:222
  39.0 3.7 %all-to-all-start.2 = ((bf16[8,64,768]{2,1,0:T(8,128)(2,1)}), bf16[8,64,768]{2,1,0:T(8,128)(2,1)S(1)}, u32[]{:S(2)}, u32[]{:S(2)}) async-start(bf16[8,64,768]{2,1,0:T(8,128)(2,1)} %get-tuple-element.23), calls=%async_computation.2 | async-start | bytes 1572864 | tf_op jit(solution)/shard_map/all_to_all | solution.py:222
  42.7 0.0 collective-permute-done.1
  42.7 1.1 broadcast_select_fusion.3.refs_6_
  43.8 0.0 copy-start.10
  43.8 0.0 collective-permute-done.3
  43.8 1.3 broadcast_select_fusion.2.refs_7_
  45.1 0.0 copy-start.12
  45.1 0.0 copy-done.15
  45.1 7.4 %own_a.1 = (bf16[512,512]{1,0:T(8,128)(2,1)S(1)}, f32[2,2304,128]{2,1,0:T(8,128)S(1)}) custom-call(s32[1]{0:T(128)} %bitcast.1.refs_0_, s32[2]{0:T(128)S(1)} %copy-done.15, bf16[512,768]{1,0:T(8,128)(2,1)S(1)} %bitcast.12, bf16[512,768]{1,0:T(8,128)(2,1)S(1)} %bitcast.13, bf16[512,768]{1,0:T(8,128)(2,1)S(1)} %bitcast.14, bf16[512,768]{1,0:T(8,128)(2,1)S(1)} %bitcast.15, ...), custom_call_target="tpu_custom_call" | custom-call | flops 3623878656 | bytes 8388608 | tf_op jit(solution)/shard_map/own_a/pallas_call | solution.py:194
  52.5 0.0 copy-start.18
  52.5 1.4 copy-done.18
  53.9 0.0 copy-done
  53.9 0.0 copy-done.10
  53.9 0.0 copy-done.12
  53.9 7.4 %lead_a.1 = (bf16[512,512]{1,0:T(8,128)(2,1)S(1)}, f32[2,2304,128]{2,1,0:T(8,128)S(1)}) custom-call(s32[1]{0:T(128)S(6)} %sub.3.refs_0_, s32[2]{0:T(128)S(1)} %copy-done.15, bf16[512,768]{1,0:T(8,128)(2,1)S(1)} %bitcast.16, bf16[512,768]{1,0:T(8,128)(2,1)S(1)} %bitcast.17, bf16[512,768]{1,0:T(8,128)(2,1)S(1)} %bitcast.18, ...), custom_call_target="tpu_custom_call", output_to_operand_aliasing={{0}: (8, {})} | custom-call | flops 3623878656 | bytes 8388608 | tf_op jit(solution)/shard_map/lead_a/pallas_call | solution.py:194
  61.3 0.0 copy-start.14
  61.3 0.8 copy-done.14
  62.1 1.4 copy-done.16
  63.6 2.7 %all-to-all-done.2 = bf16[8,64,768]{2,1,0:T(8,128)(2,1)S(1)} async-done(((bf16[8,64,768]{2,1,0:T(8,128)(2,1)}), bf16[8,64,768]{2,1,0:T(8,128)(2,1)S(1)}, u32[]{:S(2)}, u32[]{:S(2)}) %all-to-all-start.2) | async-done | bytes 786464 | tf_op jit(solution)/shard_map/all_to_all | solution.py:222
  66.2 1.0 copy-done.3
  67.2 1.1 copy-done.1
  68.3 1.1 copy-done.4
  69.5 1.0 copy-done.11
  70.5 1.0 copy-done.13
  71.5 1.7 %copy-done.17 = f32[2,2304,128]{2,1,0:T(8,128)S(1)} copy-done((f32[2,2304,128]{2,1,0:T(8,128)S(1)}, f32[2,2304,128]{2,1,0:T(8,128)}, u32[]{:S(2)}) %copy-start.17) | copy-done | bytes 2359320
  73.2 10.6 %lead_b.1 = (bf16[512,1024]{1,0:T(8,128)(2,1)S(1)}, f32[2,2304,128]{2,1,0:T(8,128)S(1)}) custom-call(s32[1]{0:T(128)S(6)} %sub.3.refs_0_, s32[2]{0:T(128)S(1)} %copy-done.15, bf16[512,768]{1,0:T(8,128)(2,1)S(1)} %bitcast.24, bf16[512,768]{1,0:T(8,128)(2,1)S(1)} %bitcast.25, bf16[512,768]{1,0:T(8,128)(2,1)S(1)} %bitcast.20, bf16[512,768]{1,0:T(8,128)(2,1)S(1)} %bitcast.21, ...), custom_call_target="tpu_custom_call" | custom-call | flops 5435817984 | bytes 8388608 | tf_op jit(solution)/shard_map/lead_b/pallas_call | solution.py:194
  83.8 1.5 slice.17
  85.3 3.8 %collective-permute-start.4 = (f32[2,2048,128]{2,1,0:T(8,128)}, f32[2,2048,128]{2,1,0:T(8,128)}, u32[]{:S(2)}, u32[]{:S(2)}) collective-permute-start(f32[2,2048,128]{2,1,0:T(8,128)} %slice.17), channel_id=1, source_target_pairs={{8,0},{24,16},{40,32},{56,48},{72,64},{88,80},{104,96},{120,112},{... | collective-permute-start | bytes 6291464 | tf_op jit(solution)/shard_map/ppermute | solution.py:237
  89.0 4.1 %all-to-all-start.1 = ((bf16[8,64,512]{2,1,0:T(8,128)(2,1)}), bf16[8,64,512]{2,1,0:T(8,128)(2,1)}, u32[]{:S(2)}, u32[]{:S(2)}) async-start(bf16[8,64,512]{2,1,0:T(8,128)(2,1)} %bitcast.34), calls=%async_computation.1 | async-start | bytes 1048576 | tf_op jit(solution)/shard_map/all_to_all | solution.py:222
  93.2 0.0 copy-start.2
  93.2 0.0 copy-start.5
  93.2 0.0 copy-start.7
  93.2 0.0 copy-start.9
  93.2 0.0 copy-start.19
  93.2 0.0 collective-permute-done.4
  93.2 3.3 %slice_add_fusion = f32[2,2048,128]{2,1,0:T(8,128)} fusion(f32[2,2048,128]{2,1,0:T(8,128)} %collective-permute-done.4, f32[2,2304,128]{2,1,0:T(8,128)S(1)} %get-tuple-element.33), kind=kLoop, calls=%fused_computation.5 | loop fusion | flops 524288 | bytes 6291456 | tf_op jit(solution)/shard_map/add | solution.py:273
  96.5 2.0 %collective-permute-start.5 = (f32[2,2048,128]{2,1,0:T(8,128)}, f32[2,2048,128]{2,1,0:T(8,128)}, u32[]{:S(2)}, u32[]{:S(2)}) collective-permute-start(f32[2,2048,128]{2,1,0:T(8,128)} %slice_add_fusion), channel_id=1, source_target_pairs={{16,0},{48,32},{80,64},{112,96},{144,128},{176,160},{208,192},{240... | collective-permute-start | bytes 6291464 | tf_op jit(solution)/shard_map/ppermute | solution.py:237
  98.6 0.0 copy-done.2
  98.6 0.0 copy-done.5
  98.6 0.0 copy-done.9
  98.6 0.0 copy-done.19
  98.6 10.6 %own_b.1 = (bf16[512,1024]{1,0:T(8,128)(2,1)S(1)}, f32[2,2304,128]{2,1,0:T(8,128)S(1)}) custom-call(s32[1]{0:T(128)} %bitcast.1.refs_0_, s32[2]{0:T(128)S(1)} %copy-done.15, bf16[512,768]{1,0:T(8,128)(2,1)S(1)} %bitcast.26, bf16[512,768]{1,0:T(8,128)(2,1)S(1)} %bitcast.27, bf16[512,768]{1,0:T(8,128)(2,1)S(1)} %bitcast.22, ...), custom_call_target="tpu_custom_call", output_to_operand_aliasing={{0}: (9, {})} | custom-call | flops 5435817984 | bytes 8388608 | tf_op jit(solution)/shard_map/own_b/pallas_call | solution.py:194
  109.2 0.3 all-to-all-done.1.a_ref
  109.4 35.4 %all_to_all.20.b_ref = bf16[8,64,1024]{2,1,0:T(8,128)(2,1)} all-to-all(bf16[8,64,1024]{2,1,0:T(8,128)(2,1)S(1)} %bitcast.11), channel_id=1, replica_groups=mesh['dp'=32,'mp'=8] {'mp'}, dimensions={0} | all-to-all | bytes 2097152 | tf_op jit(solution)/shard_map/all_to_all | solution.py:222
  144.9 5.5 %unpack.1 = (bf16[64,5120]{1,0:T(8,128)(2,1)}, bf16[64,5120]{1,0:T(8,128)(2,1)}, bf16[64,1024]{1,0:T(8,128)(2,1)}, bf16[64,1024]{1,0:T(8,128)(2,1)}) custom-call(bf16[8,64,512]{2,1,0:T(8,128)(2,1)} %all-to-all-done.1.a_ref, bf16[8,64,1024]{2,1,0:T(8,128)(2,1)} %all_to_all.20.b_ref), custom_call_target="tpu_custom_call" | custom-call | tf_op jit(solution)/shard_map/unpack/pallas_call | solution.py:81
  150.3 0.0 collective-permute-done.5
  150.3 2.5 %add_convert_fusion = bf16[2,2048,128]{2,1,0:T(8,128)(2,1)S(1)} fusion(f32[2,2048,128]{2,1,0:T(8,128)} %slice_add_fusion, f32[2,2048,128]{2,1,0:T(8,128)} %collective-permute-done.5, f32[2,2304,128]{2,1,0:T(8,128)S(1)} %get-tuple-element.32, pred[]{:T(512)S(6)} %eq.14), kind=kLoop, calls=%fused_computation | loop fusion | flops 2097152 | bytes 7340033 | tf_op jit(solution)/shard_map/convert_element_type | solution.py:276
  152.8 1.0 fusion
  (11 shorter events, 0.0 us)
Async XLA Ops:
  0.6 16.3 %copy-start.6 = (bf16[1,2048,128]{2,1,0:T(8,128)(2,1)S(1)}, bf16[1,2048,128]{2,1,0:T(8,128)(2,1)}, u32[]{:S(2)}) copy-start(bf16[1,2048,128]{2,1,0:T(8,128)(2,1)} %param.11) | copy-start | bytes 1572868
  0.6 14.8 %copy-start.8 = (bf16[1,2048,128]{2,1,0:T(8,128)(2,1)S(1)}, bf16[1,2048,128]{2,1,0:T(8,128)(2,1)}, u32[]{:S(2)}) copy-start(bf16[1,2048,128]{2,1,0:T(8,128)(2,1)} %param.12) | copy-start | bytes 1572868
  0.7 16.2 %collective-permute-start = (bf16[2048,128]{1,0:T(8,128)(2,1)}, bf16[2048,128]{1,0:T(8,128)(2,1)S(1)}, u32[]{:S(2)}, u32[]{:S(2)}) collective-permute-start(bf16[2048,128]{1,0:T(8,128)(2,1)} %bitcast.28), channel_id=1, source_target_pairs={{0,16},{32,48},{64,80},{96,112},{128,144},{160,176},{192,208},{224... | collective-permute-start | bytes 1572872 | tf_op jit(solution)/shard_map/ppermute | solution.py:237
  7.1 14.4 %copy-start.20 = (s32[2]{0:T(128)S(1)}, s32[2]{0:T(128)}, u32[]{:S(2)}) copy-start(s32[2]{0:T(128)} %param.13) | copy-start | bytes 28
  7.1 31.9 %all-to-all-start = ((bf16[8,64,768]{2,1,0:T(8,128)(2,1)}), bf16[8,64,768]{2,1,0:T(8,128)(2,1)S(1)}, u32[]{:S(2)}, u32[]{:S(2)}) async-start(bf16[8,64,768]{2,1,0:T(8,128)(2,1)} %get-tuple-element.20), calls=%async_computation | async-start | bytes 1572864 | tf_op jit(solution)/shard_map/all_to_all | solution.py:222
  15.4 2.8 %collective-permute-start.2 = (bf16[2048,128]{1,0:T(8,128)(2,1)S(1)}, bf16[2048,128]{1,0:T(8,128)(2,1)}, u32[]{:S(2)}, u32[]{:S(2)}) collective-permute-start(bf16[2048,128]{1,0:T(8,128)(2,1)S(1)} %bitcast.31), channel_id=1, source_target_pairs={{0,16},{32,48},{64,80},{96,112},{128,144},{160,176},{192,208},{224... | collective-permute-start | bytes 1572872 | tf_op jit(solution)/shard_map/ppermute | solution.py:237
  17.0 25.7 %collective-permute-start.1 = (bf16[2048,128]{1,0:T(8,128)(2,1)S(1)}, bf16[2048,128]{1,0:T(8,128)(2,1)}, u32[]{:S(2)}, u32[]{:S(2)}) collective-permute-start(bf16[2048,128]{1,0:T(8,128)(2,1)S(1)} %broadcast_select_fusion.1), channel_id=1, source_target_pairs={{0,8},{16,24},{32,40},{48,56},{64,72},{80,88},{96,104},{112,120},{... | collective-permute-start | bytes 1572872 | tf_op jit(solution)/shard_map/ppermute | solution.py:237
  20.2 23.6 %collective-permute-start.3 = (bf16[2048,128]{1,0:T(8,128)(2,1)}, bf16[2048,128]{1,0:T(8,128)(2,1)}, u32[]{:S(2)}, u32[]{:S(2)}) collective-permute-start(bf16[2048,128]{1,0:T(8,128)(2,1)} %broadcast_select_fusion), channel_id=1, source_target_pairs={{0,8},{16,24},{32,40},{48,56},{64,72},{80,88},{96,104},{112,120},{... | collective-permute-start | bytes 1572872 | tf_op jit(solution)/shard_map/ppermute | solution.py:237
  39.0 14.9 %copy-start = (bf16[8,64,768]{2,1,0:T(8,128)(2,1)}, bf16[8,64,768]{2,1,0:T(8,128)(2,1)S(1)}, u32[]{:S(2)}) copy-start(bf16[8,64,768]{2,1,0:T(8,128)(2,1)S(1)} %all-to-all-done) | copy-start | bytes 2359300
  39.0 6.1 %copy-start.15 = (s32[2]{0:T(128)S(1)}, s32[2]{0:T(128)}, u32[]{:S(2)}) copy-start(s32[2]{0:T(128)} %refs_1_.7) | copy-start | bytes 28
  39.0 27.2 %all-to-all-start.2 = ((bf16[8,64,768]{2,1,0:T(8,128)(2,1)}), bf16[8,64,768]{2,1,0:T(8,128)(2,1)S(1)}, u32[]{:S(2)}, u32[]{:S(2)}) async-start(bf16[8,64,768]{2,1,0:T(8,128)(2,1)} %get-tuple-element.23), calls=%async_computation.2 | async-start | bytes 1572864 | tf_op jit(solution)/shard_map/all_to_all | solution.py:222
  43.8 10.1 %copy-start.10 = (bf16[2048,128]{1,0:T(8,128)(2,1)}, bf16[2048,128]{1,0:T(8,128)(2,1)S(1)}, u32[]{:S(2)}) copy-start(bf16[2048,128]{1,0:T(8,128)(2,1)S(1)} %broadcast_select_fusion.3.refs_6_) | copy-start | bytes 1572868
  45.1 8.8 %copy-start.12 = (bf16[2048,128]{1,0:T(8,128)(2,1)}, bf16[2048,128]{1,0:T(8,128)(2,1)S(1)}, u32[]{:S(2)}) copy-start(bf16[2048,128]{1,0:T(8,128)(2,1)S(1)} %broadcast_select_fusion.2.refs_7_) | copy-start | bytes 1572868
  52.5 1.4 copy-start.18
  61.3 0.8 copy-start.14
  62.1 1.4 copy-start.16
  66.2 1.0 copy-start.3
  67.2 1.1 copy-start.1
  68.3 1.1 copy-start.4
  69.5 1.0 copy-start.11
  70.5 1.0 copy-start.13
  71.5 1.7 %copy-start.17 = (f32[2,2304,128]{2,1,0:T(8,128)S(1)}, f32[2,2304,128]{2,1,0:T(8,128)}, u32[]{:S(2)}) copy-start(f32[2,2304,128]{2,1,0:T(8,128)} %copy-done.16) | copy-start | bytes 7077892
  85.3 8.0 %collective-permute-start.4 = (f32[2,2048,128]{2,1,0:T(8,128)}, f32[2,2048,128]{2,1,0:T(8,128)}, u32[]{:S(2)}, u32[]{:S(2)}) collective-permute-start(f32[2,2048,128]{2,1,0:T(8,128)} %slice.17), channel_id=1, source_target_pairs={{8,0},{24,16},{40,32},{56,48},{72,64},{88,80},{104,96},{120,112},{... | collective-permute-start | bytes 6291464 | tf_op jit(solution)/shard_map/ppermute | solution.py:237
  89.0 20.4 %all-to-all-start.1 = ((bf16[8,64,512]{2,1,0:T(8,128)(2,1)}), bf16[8,64,512]{2,1,0:T(8,128)(2,1)}, u32[]{:S(2)}, u32[]{:S(2)}) async-start(bf16[8,64,512]{2,1,0:T(8,128)(2,1)} %bitcast.34), calls=%async_computation.1 | async-start | bytes 1048576 | tf_op jit(solution)/shard_map/all_to_all | solution.py:222
  93.2 5.4 %copy-start.2 = (bf16[8,64,768]{2,1,0:T(8,128)(2,1)S(1)}, bf16[8,64,768]{2,1,0:T(8,128)(2,1)}, u32[]{:S(2)}) copy-start(bf16[8,64,768]{2,1,0:T(8,128)(2,1)} %copy-done) | copy-start | bytes 2359300
  93.2 5.4 %copy-start.5 = (bf16[8,64,768]{2,1,0:T(8,128)(2,1)S(1)}, bf16[8,64,768]{2,1,0:T(8,128)(2,1)}, u32[]{:S(2)}) copy-start(bf16[8,64,768]{2,1,0:T(8,128)(2,1)} %copy-done.3) | copy-start | bytes 2359300
  93.2 5.4 %copy-start.7 = (bf16[1,2048,128]{2,1,0:T(8,128)(2,1)S(1)}, bf16[1,2048,128]{2,1,0:T(8,128)(2,1)}, u32[]{:S(2)}) copy-start(bf16[1,2048,128]{2,1,0:T(8,128)(2,1)} %param.11) | copy-start | bytes 1572868
  93.2 5.4 %copy-start.9 = (bf16[1,2048,128]{2,1,0:T(8,128)(2,1)S(1)}, bf16[1,2048,128]{2,1,0:T(8,128)(2,1)}, u32[]{:S(2)}) copy-start(bf16[1,2048,128]{2,1,0:T(8,128)(2,1)} %param.12) | copy-start | bytes 1572868
  93.2 5.4 %copy-start.19 = (f32[2,2304,128]{2,1,0:T(8,128)S(1)}, f32[2,2304,128]{2,1,0:T(8,128)}, u32[]{:S(2)}) copy-start(f32[2,2304,128]{2,1,0:T(8,128)} %copy-done.18) | copy-start | bytes 7077892
  96.5 53.8 %collective-permute-start.5 = (f32[2,2048,128]{2,1,0:T(8,128)}, f32[2,2048,128]{2,1,0:T(8,128)}, u32[]{:S(2)}, u32[]{:S(2)}) collective-permute-start(f32[2,2048,128]{2,1,0:T(8,128)} %slice_add_fusion), channel_id=1, source_target_pairs={{16,0},{48,32},{80,64},{112,96},{144,128},{176,160},{208,192},{240... | collective-permute-start | bytes 6291464 | tf_op jit(solution)/shard_map/ppermute | solution.py:237

commit v2 on v0

v2 whole, which is shorter than its diff:
```python
import functools

import jax
import jax.numpy as jnp
from jax import lax
from jax.experimental import pallas as pl
from jax.experimental.pallas import tpu as pltpu
from jax.sharding import PartitionSpec as P

HD = 128
GROUP = 5
REACH = 4
CLEN = 256
PREFIX = 2048
CHUNK = 256
STEPS = PREFIX // CHUNK + 1
KEYS = PREFIX + CLEN
ROWS = 64
QUAD = 4
COLS = GROUP * CLEN
WIDE = GROUP * HD
PARTS = 8
SEND = 2 * WIDE + 2 * HD
SCALE = HD**-0.5
SCALE_LOG2E = SCALE * 1.4426950408889634
MASKED = -1e30
F32 = jnp.float32
BF16 = jnp.bfloat16
PIECE = PREFIX // 4
ANY = pl.BlockSpec(memory_space=pl.ANY)


def nt(a, b):
    return lax.dot_general(a, b, (((1,), (1,)), ((), ())), preferred_element_type=F32)


def nn(a, b):
    return lax.dot_general(a, b, (((1,), (0,)), ((), ())), preferred_element_type=F32)


def head_columns(part, width):
    return pl.ds(pl.multiple_of(part * width, HD), width)


def pack_kernel(q, k, v, g, pk, pv, prefix, out):
    prefix[0] = pk[...]
    prefix[1] = pv[...]
    for m in range(PARTS):
        wide, thin = slice(m * WIDE, (m + 1) * WIDE), slice(m * HD, (m + 1) * HD)
        out[m, :, :WIDE] = q[:, wide]
        out[m, :, WIDE : 2 * WIDE] = g[:, wide]
        out[m, :, 2 * WIDE : 2 * WIDE + HD] = k[:, thin]
        out[m, :, 2 * WIDE + HD :] = v[:, thin]


def pack(q, k, v, g, pk, pv):
    vmem = pl.BlockSpec(memory_space=pltpu.VMEM)
    return pl.pallas_call(
        pack_kernel,
        in_specs=[vmem] * 6,
        out_specs=[vmem] * 2,
        out_shape=[
            jax.ShapeDtypeStruct((2, PREFIX, HD), BF16),
            jax.ShapeDtypeStruct((PARTS, ROWS, SEND), BF16),
        ],
        name="pack",
    )(q, k, v, g, pk, pv)


def unpack_kernel(ids, *refs):
    bufs, (o, dq, dk, dv) = refs[:PARTS], refs[PARTS:]
    me = ids[1]
    for p in range(PARTS):
        cols = head_columns(me ^ p, WIDE)
        o[:, cols] = bufs[p][:, :WIDE]
        dq[:, cols] = bufs[p][:, WIDE : 2 * WIDE]
        cols = head_columns(me ^ p, HD)
        dk[:, cols] = bufs[p][:, 2 * WIDE : 2 * WIDE + HD]
        dv[:, cols] = bufs[p][:, 2 * WIDE + HD :]


def unpack(ids, bufs):
    vmem = pl.BlockSpec(memory_space=pltpu.VMEM)
    wide = jax.ShapeDtypeStruct((ROWS, PARTS * WIDE), BF16)
    thin = jax.ShapeDtypeStruct((ROWS, PARTS * HD), BF16)
    return pl.pallas_call(
        unpack_kernel,
        in_specs=[pl.BlockSpec(memory_space=pltpu.SMEM)] + [vmem] * PARTS,
        out_specs=[vmem] * 4,
        out_shape=[wide, wide, thin, thin],
        cost_estimate=pl.CostEstimate(flops=1 << 36, bytes_accessed=4 << 20, transcendentals=0),
        name="unpack",
    )(ids, *bufs)


def attend_kernel(far, chained, ids, prompt_of, lengths, *refs):
    bufs, refs = refs[0], refs[1:]
    pk, pv, far_prefix, near_prefix = refs[:4]
    refs = refs[4 + 2 * chained :]
    outs, refs = refs[:QUAD], refs[QUAD:]
    own_ref, lead_ref, q_ref, g_ref, k_own, v_own, e_ref, w_ref, d_ref = refs[:9]
    kt_ref, vt_ref, move_ref, pre_ref, acc_ref, pre_sem, acc_sem = refs[9:]
    dp_at, part = ids[0], ids[1]
    slot = (part >> 2) ^ far
    length = lengths[slot]
    role = jnp.where(slot == jnp.where(prompt_of[0] == dp_at, 0, 1), 0, 1)
    place = dp_at & 3
    source = jnp.where((role == 0) | (place == 0), 0, jnp.where(place == 2, 1, 2))
    places = [((part ^ n) & 3) * ROWS for n in range(QUAD)]

    def token_rows(n):
        return pl.ds(pl.multiple_of(places[n], ROWS), ROWS)

    sources = ((pk, pv), *((x.at[0], x.at[1]) for x in (far_prefix, near_prefix)))

    def prefix_copy(n, source_refs):
        return pltpu.make_async_copy(source_refs[n], pre_ref.at[n], pre_sem.at[n])

    for number, source_refs in enumerate(sources):

        @pl.when(source == number)
        def _(source_refs=source_refs):
            prefix_copy(0, source_refs).start()
            prefix_copy(1, source_refs).start()

    def key_rows(i):
        return k_own[...] if i == STEPS - 1 else pre_ref[0, rows[i], :]

    def value_rows(i):
        return v_own[...] if i == STEPS - 1 else pre_ref[1, rows[i], :]

    zero = jnp.zeros((), BF16)
    row = lax.broadcasted_iota(jnp.int32, (ROWS, HD), 0)
    for n in range(QUAD):
        live = n * ROWS + row < length
        k_own[n * ROWS : (n + 1) * ROWS, :] = bufs[n, :, 2 * WIDE : 2 * WIDE + HD]
        v_own[n * ROWS : (n + 1) * ROWS, :] = bufs[n, :, 2 * WIDE + HD :]
        for h in range(GROUP):
            at = slice(h * CLEN + n * ROWS, h * CLEN + (n + 1) * ROWS)
            q_ref[at, :] = bufs[n, :, h * HD : (h + 1) * HD]
            g_ref[at, :] = jnp.where(live, bufs[n, :, WIDE + h * HD : WIDE + (h + 1) * HD], zero)

    cols = [slice(h * CLEN, (h + 1) * CLEN) for h in range(GROUP)]
    rows = [slice(i * CHUNK, (i + 1) * CHUNK) for i in range(STEPS)]
    order = [STEPS - 1, *range(STEPS - 1)]
    tops, sums = [[] for _ in cols], [[] for _ in cols]
    scales, delta = [None] * GROUP, [None] * GROUP

    def scores(h, i):
        s = nt(key_rows(i), q_ref[cols[h], :])
        if i == STEPS - 1:
            key_at = lax.broadcasted_iota(jnp.int32, (CHUNK, CLEN), 0)
            query_at = lax.broadcasted_iota(jnp.int32, (CHUNK, CLEN), 1)
            s = jnp.where((key_at <= query_at) & (key_at < length), s, MASKED)
        top = jnp.max(s, 0, keepdims=True)
        e = jnp.exp2((s - top) * SCALE_LOG2E)
        e_ref[rows[i], cols[h]] = e
        tops[h].append(top)
        sums[h].append(jnp.sum(e, 0, keepdims=True))

    def normalise(h):
        best = functools.reduce(jnp.maximum, tops[h])
        parts = [jnp.exp2((t - best) * SCALE_LOG2E) for t in tops[h]]
        inv = 1.0 / functools.reduce(jnp.add, [f * s for f, s in zip(parts, sums[h])])
        scales[h] = {i: f * inv for i, f in zip(order, parts)}

    def give(column, x):
        move_ref[...] = x
        for n in range(QUAD):
            outs[n][:, column * HD : (column + 1) * HD] = move_ref[token_rows(n), :]

    def weigh(h, i):
        w_ref[rows[i], cols[h]] = (e_ref[rows[i], cols[h]] * scales[h][i]).astype(BF16)

    def attended(h):
        ob = nn(vt_ref[...], w_ref[:, cols[h]]).astype(BF16)
        gt = g_ref[cols[h], :].T
        delta[h] = jnp.sum(gt.astype(F32) * ob.astype(F32), 0, keepdims=True)
        give(h, ob.T)

    def d_scores(h, i):
        dp = nt(value_rows(i), g_ref[cols[h], :])
        probs = e_ref[rows[i], cols[h]] * scales[h][i]
        d_ref[rows[i], cols[h]] = (probs * (dp - delta[h])).astype(BF16)

    def d_queries(h):
        give(GROUP + h, (nn(kt_ref[...], d_ref[:, cols[h]]) * SCALE).astype(BF16).T)

    for n in range(GROUP + 2):
        for i in order:
            if n < 2 and i == 0:
                prefix_copy(n, sources[0]).wait()
            if n == 0:
                kt_ref[:, rows[i]] = key_rows(i).T
            if n == 1:
                vt_ref[:, rows[i]] = value_rows(i).T
            if n < GROUP:
                scores(n, i)
            if 1 <= n <= GROUP:
                weigh(n - 1, i)
            if n >= 2:
                d_scores(n - 2, i)
        if n < GROUP:
            normalise(n)
        if 1 <= n <= GROUP:
            attended(n - 1)
        if n >= 2:
            d_queries(n - 2)

    def store_copy(n, target):
        piece = pl.ds(n * PIECE, PIECE)
        return pltpu.make_async_copy(acc_ref.at[:, piece, :], target.at[:, piece, :], acc_sem.at[n])

    for i in order:
        dk = nn(d_ref[rows[i], :], q_ref[...]) * SCALE
        dv = nn(w_ref[rows[i], :], g_ref[...])
        if i == STEPS - 1:
            give(2 * GROUP, dk.astype(BF16))
            give(2 * GROUP + 1, dv.astype(BF16))
            continue
        acc_ref[0, rows[i], :] = dk
        acc_ref[1, rows[i], :] = dv
        if i % 2 == 1:

            @pl.when(role == 0)
            def _():
                store_copy(i // 2, own_ref).start()

            @pl.when(role == 1)
            def _():
                store_copy(i // 2, lead_ref).start()

    for n in range(4):
        store_copy(n, own_ref).wait()


def attend(name, far, scalars, rows, prefix, leads, chain=()):
    whole = pl.BlockSpec((ROWS, SEND), lambda n, *_: (0, 0))
    quad = pl.BlockSpec((QUAD, ROWS, SEND), lambda n, ids, *_: ((ids[1] >> 2) ^ far, 0, 0))
    args = [rows, *prefix, *leads, *chain]
    grads = jax.ShapeDtypeStruct((2, PREFIX, HD), F32)
    return pl.pallas_call(
        functools.partial(attend_kernel, far, len(chain) > 0),
        grid_spec=pltpu.PrefetchScalarGridSpec(
            num_scalar_prefetch=3,
            grid=(1,),
            in_specs=[quad] + [ANY] * (4 + len(chain)),
            out_specs=[whole] * QUAD + [ANY] * 2,
            scratch_shapes=[
                pltpu.VMEM((COLS, HD), BF16),
                pltpu.VMEM((COLS, HD), BF16),
                pltpu.VMEM((CLEN, HD), BF16),
                pltpu.VMEM((CLEN, HD), BF16),
                pltpu.VMEM((KEYS, COLS), F32),
                pltpu.VMEM((KEYS, COLS), BF16),
                pltpu.VMEM((KEYS, COLS), BF16),
                pltpu.VMEM((HD, KEYS), BF16),
                pltpu.VMEM((HD, KEYS), BF16),
                pltpu.VMEM((CLEN, HD), BF16),
                pltpu.VMEM((2, PREFIX, HD), BF16),
                pltpu.VMEM((2, PREFIX, HD), F32),
                pltpu.SemaphoreType.DMA((2,)),
                pltpu.SemaphoreType.DMA((4,)),
            ],
        ),
        out_shape=[jax.ShapeDtypeStruct((ROWS, SEND), BF16)] * QUAD + [grads] * 2,
        input_output_aliases={3 + len(args) - 2 + n: QUAD + n for n in range(len(chain))},
        compiler_params=pltpu.CompilerParams(vmem_limit_bytes=62 * 1024 * 1024),
        cost_estimate=pl.CostEstimate(flops=1 << 20, bytes_accessed=1 << 16, transcendentals=0),
        name=name,
    )(*scalars, *args)


def local(queries, keys, values, prefix_keys, prefix_values, prompt_of, lengths, cotangent):
    groups = lax.axis_size("dp") // REACH
    me, part = lax.axis_index("dp"), lax.axis_index("mp")
    pk, pv = prefix_keys[0], prefix_values[0]
    ids = jnp.stack([me, part]).astype(jnp.int32)
    scalars = (ids, prompt_of, lengths)

    def send(x, *pairs):
        return lax.ppermute(
            x, "dp", [(REACH * n + a, REACH * n + b) for n in range(groups) for a, b in pairs]
        )

    def swap(x, p):
        return lax.ppermute(x, "mp", [(i, i ^ p) for i in range(PARTS)])

    prefix, rows = pack(queries, keys, values, cotangent, pk, pv)
    leader = me % REACH == 0
    far = send(prefix, (0, 2))
    near = send(jnp.where(leader, prefix, far), (0, 1), (2, 3))
    leads = (far, near)
    rows = lax.all_to_all(rows, "mp", split_axis=0, concat_axis=0, tiled=True)
    *back_far, own_grads, lead_grads = attend("far", 1, scalars, rows, (pk, pv), leads)
    *back_near, own_grads, lead_grads = attend(
        "near", 0, scalars, rows, (pk, pv), leads, (own_grads, lead_grads)
    )
    back = back_near + back_far
    back = [back[0]] + [swap(back[p], p) for p in range(1, PARTS)]

    lead_grads, *back[4:6] = lax.optimization_barrier((lead_grads, *back[4:6]))
    near_sum = lead_grads + send(lead_grads, (1, 0), (3, 2))
    far_grads = send(near_sum.astype(BF16), (2, 0))
    base = own_grads + jnp.where(leader, near_sum, 0.0)
    d_keys, d_values = (
        (base[n] + far_grads[n].astype(F32)).astype(BF16)[None] for n in range(2)
    )
    outs = unpack(ids, back)
    return (*outs, d_keys, d_values)


def solution(mesh):
    rows = P(("dp", "mp"), None)
    heads = P("dp", None, "mp")
    return jax.shard_map(
        local,
        mesh=mesh,
        in_specs=(rows, rows, rows, heads, heads, P("dp"), P("dp"), rows),
        out_specs=(rows, rows, rows, rows, heads, heads),
        check_vma=False,
    )
```

time: 492 us -> 124 us (0.25)
  the two profiles are of different devices: /device:TPU:61 before, /device:TPU:1 now
where the time goes in v2:
time: 124 us; the launch traced here: 123 us
  waiting for transfers between devices  49.2 us (40%)
  Pallas kernels  35.9 us (29%)
  starting transfers between devices  26.8 us (22%)
  other arithmetic  6.8 us (5%)
  local copies, waits for them, and re-layouts  3.91 us (3%)
    pallas_call x2, Pallas kernels, attend(): pl.pallas_call(functools.partial(attend_kernel, far, len(chain) > 0), gri...  29.8 us
    ppermute x4, waiting for transfers between devices, send(): lax.ppermute(x, 'dp', [(REACH * n + a, REACH * n + b) for n in range(grou...  19.6 us
    ppermute x7, waiting for transfers between devices, swap(): return lax.ppermute(x, 'mp', [(i, i ^ p) for i in range(PARTS)])  14.9 us
    all_to_all x1, waiting for transfers between devices, local(): rows = lax.all_to_all(rows, 'mp', split_axis=0, concat_axis=0, tiled=True)  14.8 us
    ppermute x7, starting transfers between devices, swap(): return lax.ppermute(x, 'mp', [(i, i ^ p) for i in range(PARTS)])  11.2 us
    all_to_all x1, starting transfers between devices, local(): rows = lax.all_to_all(rows, 'mp', split_axis=0, concat_axis=0, tiled=True)  9.01 us
    ppermute x4, starting transfers between devices, send(): lax.ppermute(x, 'dp', [(REACH * n + a, REACH * n + b) for n in range(grou...  6.57 us
    unnamed x18, local copies, waits for them, and re-layouts  3.91 us
  transfers between devices with their start and end apart: 12, of which 6 were waited for; matrix products, arithmetic and copies ran while one was open for 4% of the time, Pallas kernels for 14%

profile of v2, /device:TPU:1, one launch (start us, length us, event | category | flops | bytes accessed | tf_op | source)
XLA Modules:
  0.0 123.4 jit_solution(4428922669658422208)
XLA Ops:
  0.6 3.3 %pack.1 = (bf16[2,2048,128]{2,1,0:T(8,128)(2,1)}, bf16[8,64,1536]{2,1,0:T(8,128)(2,1)}) custom-call(bf16[64,5120]{1,0:T(8,128)(2,1)} %q.1, bf16[64,1024]{1,0:T(8,128)(2,1)} %k.1, bf16[64,1024]{1,0:T(8,128)(2,1)} %v.1, bf16[64,5120]{1,0:T(8,128)(2,1)} %g.1, bf16[2048,128]{1,0:T(8,128)(2,1)} %bitcast.4, bf16[2048,128]{1,0:T(8,128)(2,1)} %bitcast.7), custom_call_target="tpu_custom_call" | custom-call | tf_op jit(solution)/shard_map/pack/pallas_call | solution.py:58
  4.0 9.0 %all-to-all-start = ((bf16[8,64,1536]{2,1,0:T(8,128)(2,1)}), bf16[8,64,1536]{2,1,0:T(8,128)(2,1)S(1)}, u32[]{:S(2)}, u32[]{:S(2)}) async-start(bf16[8,64,1536]{2,1,0:T(8,128)(2,1)} %get-tuple-element.27), calls=%async_computation | async-start | bytes 3145728 | tf_op jit(solution)/shard_map/all_to_all | solution.py:294
  13.0 0.7 collective-permute-start
  13.7 0.0 collective-permute-done.refs_3_
  13.7 0.0 copy-start.1
  13.7 1.2 broadcast_select_fusion
  14.9 1.3 %collective-permute-start.1 = (bf16[2,2048,128]{2,1,0:T(8,128)(2,1)}, bf16[2,2048,128]{2,1,0:T(8,128)(2,1)}, u32[]{:S(2)}, u32[]{:S(2)}) collective-permute-start(bf16[2,2048,128]{2,1,0:T(8,128)(2,1)} %broadcast_select_fusion), channel_id=1, source_target_pairs={{0,8},{16,24},{32,40},{48,56},{64,72},{80,88},{96,104},{112,120},{... | collective-permute-start | bytes 3145736 | tf_op jit(solution)/shard_map/ppermute | solution.py:282
  16.2 0.7 pad_add_fusion.ids
  16.9 0.0 copy-done.1
  16.9 19.6 %collective-permute-done.1.refs_4_ = bf16[2,2048,128]{2,1,0:T(8,128)(2,1)} collective-permute-done((bf16[2,2048,128]{2,1,0:T(8,128)(2,1)}, bf16[2,2048,128]{2,1,0:T(8,128)(2,1)}, u32[]{:S(2)}, u32[]{:S(2)}) %collective-permute-start.1) | collective-permute-done | bytes 1048608 | tf_op jit(solution)/shard_map/ppermute | solution.py:282
  36.5 14.8 %all-to-all-done.refs_0_ = bf16[8,64,1536]{2,1,0:T(8,128)(2,1)S(1)} async-done(((bf16[8,64,1536]{2,1,0:T(8,128)(2,1)}), bf16[8,64,1536]{2,1,0:T(8,128)(2,1)S(1)}, u32[]{:S(2)}, u32[]{:S(2)}) %all-to-all-start) | async-done | bytes 1572896 | tf_op jit(solution)/shard_map/all_to_all | solution.py:294
  51.2 0.0 copy-start
  51.2 1.2 copy-done
  52.4 14.9 %far.1 = (bf16[64,1536]{1,0:T(8,128)(2,1)}, bf16[64,1536]{1,0:T(8,128)(2,1)}, bf16[64,1536]{1,0:T(8,128)(2,1)}, bf16[64,1536]{1,0:T(8,128)(2,1)}, f32[2,2048,128]{2,1,0:T(8,128)}, /*index=5*/f32[2,2048,128]{2,1,0:T(8,128)}) custom-call(s32[2]{0:T(128)} %pad_add_fusion.ids, s32[2]{0:T(128)} %prompt_of.3, s32[2]{0:T(128)} %lengths.3, ...), custom_call_target="tpu_custom_call" | custom-call | flops 1048576 | bytes 65536 | tf_op jit(solution)/shard_map/far/pallas_call | solution.py:242
  67.3 0.3 collective-permute-start.5
  67.6 5.0 %collective-permute-start.6 = (bf16[64,1536]{1,0:T(8,128)(2,1)}, bf16[64,1536]{1,0:T(8,128)(2,1)S(1)}, u32[]{:S(2)}, u32[]{:S(2)}) collective-permute-start(bf16[64,1536]{1,0:T(8,128)(2,1)} %get-tuple-element.37), channel_id=1, source_target_pairs={{0,5},{1,4},{2,7},{3,6},{4,1},{5,0},{6,3},{7,2},{8,13},{9,12},{10,... | collective-permute-start | bytes 589832 | tf_op jit(solution)/shard_map/ppermute | solution.py:287
  72.6 15.0 %near.1 = (bf16[64,1536]{1,0:T(8,128)(2,1)}, bf16[64,1536]{1,0:T(8,128)(2,1)}, bf16[64,1536]{1,0:T(8,128)(2,1)}, bf16[64,1536]{1,0:T(8,128)(2,1)}, f32[2,2048,128]{2,1,0:T(8,128)}, /*index=5*/f32[2,2048,128]{2,1,0:T(8,128)}) custom-call(s32[2]{0:T(128)} %pad_add_fusion.ids, s32[2]{0:T(128)} %prompt_of.3, ...), custom_call_target="tpu_custom_call", output_to_operand_aliasing={{4}: (8, {}), {5}: (9, {})} | custom-call | flops 1048576 | bytes 65536 | tf_op jit(solution)/shard_map/near/pallas_call | solution.py:242
  87.5 0.0 collective-permute-done.5.refs_4_
  87.5 0.0 copy-start.2
  87.6 2.1 %collective-permute-done.6.refs_5_ = bf16[64,1536]{1,0:T(8,128)(2,1)S(1)} collective-permute-done((bf16[64,1536]{1,0:T(8,128)(2,1)}, bf16[64,1536]{1,0:T(8,128)(2,1)S(1)}, u32[]{:S(2)}, u32[]{:S(2)}) %collective-permute-start.6) | collective-permute-done | bytes 196640 | tf_op jit(solution)/shard_map/ppermute | solution.py:287
  89.7 0.0 copy-start.3
  89.7 3.0 %collective-permute-start.9 = (f32[2,2048,128]{2,1,0:T(8,128)}, f32[2,2048,128]{2,1,0:T(8,128)S(1)}, u32[]{:S(2)}, u32[]{:S(2)}) collective-permute-start(f32[2,2048,128]{2,1,0:T(8,128)} %get-tuple-element.47), channel_id=1, source_target_pairs={{8,0},{24,16},{40,32},{56,48},{72,64},{88,80},{104,96},{120,112},{... | collective-permute-start | bytes 6291464 | tf_op jit(solution)/shard_map/ppermute | solution.py:282
  92.7 0.9 collective-permute-start.2
  93.6 0.3 collective-permute-start.3
  93.9 2.4 %collective-permute-start.4 = (bf16[64,1536]{1,0:T(8,128)(2,1)}, bf16[64,1536]{1,0:T(8,128)(2,1)S(1)}, u32[]{:S(2)}, u32[]{:S(2)}) collective-permute-start(bf16[64,1536]{1,0:T(8,128)(2,1)} %get-tuple-element.34), channel_id=1, source_target_pairs={{0,3},{1,2},{2,1},{3,0},{4,7},{5,6},{6,5},{7,4},{8,11},{9,10},{10,... | collective-permute-start | bytes 589832 | tf_op jit(solution)/shard_map/ppermute | solution.py:287
  96.3 0.2 collective-permute-start.7
  96.5 0.0 collective-permute-done.9
  96.6 2.1 %collective-permute-start.8 = (bf16[64,1536]{1,0:T(8,128)(2,1)}, bf16[64,1536]{1,0:T(8,128)(2,1)S(1)}, u32[]{:S(2)}, u32[]{:S(2)}) collective-permute-start(bf16[64,1536]{1,0:T(8,128)(2,1)} %get-tuple-element.41), channel_id=1, source_target_pairs={{0,7},{1,6},{2,5},{3,4},{4,3},{5,2},{6,1},{7,0},{8,15},{9,14},{10,... | collective-permute-start | bytes 589832 | tf_op jit(solution)/shard_map/ppermute | solution.py:287
  98.6 2.6 %add_convert_fusion = (bf16[2,2048,128]{2,1,0:T(8,128)(2,1)S(1)}, f32[2,2048,128]{2,1,0:T(8,128)S(1)}) fusion(f32[2,2048,128]{2,1,0:T(8,128)} %get-tuple-element.47, f32[2,2048,128]{2,1,0:T(8,128)S(1)} %collective-permute-done.9, f32[2,2048,128]{2,1,0:T(8,128)} %get-tuple-element.46, pred[]{:T(512)S(6)} %eq.5), kind=kLoop, calls=%fused_computation.6 | loop fusion | flops 2097152 | bytes 9437185 | tf_op jit(solution)/shard_map/convert_element_type | solution.py:304
  101.2 0.0 copy-done.2
  101.2 0.0 copy-done.3
  101.2 2.9 %collective-permute-done.2.refs_1_ = bf16[64,1536]{1,0:T(8,128)(2,1)S(1)} collective-permute-done((bf16[64,1536]{1,0:T(8,128)(2,1)}, bf16[64,1536]{1,0:T(8,128)(2,1)S(1)}, u32[]{:S(2)}, u32[]{:S(2)}) %collective-permute-start.2) | collective-permute-done | bytes 196640 | tf_op jit(solution)/shard_map/ppermute | solution.py:287
  104.1 0.0 copy-start.4
  104.1 1.6 %collective-permute-start.10 = (bf16[2,2048,128]{2,1,0:T(8,128)(2,1)S(1)}, bf16[2,2048,128]{2,1,0:T(8,128)(2,1)}, u32[]{:S(2)}, u32[]{:S(2)}) collective-permute-start(bf16[2,2048,128]{2,1,0:T(8,128)(2,1)S(1)} %get-tuple-element.48), channel_id=1, source_target_pairs={{16,0},{48,32},{80,64},{112,96},{144,128},{176,160},{208,192},{240... | collective-permute-start | bytes 3145736 | tf_op jit(solution)/shard_map/ppermute | solution.py:282
  105.7 0.0 copy-done.4
  105.7 0.6 collective-permute-done.3.refs_2_
  106.3 0.0 copy-start.5
  106.3 0.7 copy-done.5
  107.0 9.3 %collective-permute-done.4.refs_3_ = bf16[64,1536]{1,0:T(8,128)(2,1)S(1)} collective-permute-done((bf16[64,1536]{1,0:T(8,128)(2,1)}, bf16[64,1536]{1,0:T(8,128)(2,1)S(1)}, u32[]{:S(2)}, u32[]{:S(2)}) %collective-permute-start.4) | collective-permute-done | bytes 196640 | tf_op jit(solution)/shard_map/ppermute | solution.py:287
  116.2 0.0 copy-start.6
  116.2 0.7 copy-done.6
  116.9 0.0 collective-permute-done.7.refs_6_
  116.9 0.0 copy-start.7
  116.9 0.7 copy-done.7
  117.6 0.0 collective-permute-done.8.refs_7_
  117.6 0.0 copy-start.8
  117.6 0.7 copy-done.8
  118.3 2.8 %unpack.1 = (bf16[64,5120]{1,0:T(8,128)(2,1)}, bf16[64,5120]{1,0:T(8,128)(2,1)}, bf16[64,1024]{1,0:T(8,128)(2,1)}, bf16[64,1024]{1,0:T(8,128)(2,1)}) custom-call(s32[2]{0:T(128)} %pad_add_fusion.ids, bf16[64,1536]{1,0:T(8,128)(2,1)} %get-tuple-element.31.refs_0_, bf16[64,1536]{1,0:T(8,128)(2,1)} %copy-done.4, bf16[64,1536]{1,0:T(8,128)(2,1)} %copy-done.5, ...), custom_call_target="tpu_custom_call" | custom-call | flops 68719476736 | bytes 4194304 | tf_op jit(solution)/shard_map/unpack/pallas_call | solution.py:86
  121.0 0.0 collective-permute-done.10
  121.0 2.4 %fusion = (bf16[1,2048,128]{2,1,0:T(8,128)(2,1)}, bf16[1,2048,128]{2,1,0:T(8,128)(2,1)}) fusion(f32[2,2048,128]{2,1,0:T(8,128)S(1)} %get-tuple-element.49, bf16[2,2048,128]{2,1,0:T(8,128)(2,1)} %collective-permute-done.10), kind=kLoop, calls=%fused_computation.2 | loop fusion | flops 1572864 | bytes 4194304 | tf_op jit(solution)/shard_map/convert_element_type | solution.py:307
Async XLA Ops:
  4.0 47.3 %all-to-all-start = ((bf16[8,64,1536]{2,1,0:T(8,128)(2,1)}), bf16[8,64,1536]{2,1,0:T(8,128)(2,1)S(1)}, u32[]{:S(2)}, u32[]{:S(2)}) async-start(bf16[8,64,1536]{2,1,0:T(8,128)(2,1)} %get-tuple-element.27), calls=%async_computation | async-start | bytes 3145728 | tf_op jit(solution)/shard_map/all_to_all | solution.py:294
  13.0 0.7 collective-permute-start
  13.7 3.2 %copy-start.1 = (bf16[2,2048,128]{2,1,0:T(8,128)(2,1)}, bf16[2,2048,128]{2,1,0:T(8,128)(2,1)S(1)}, u32[]{:S(2)}) copy-start(bf16[2,2048,128]{2,1,0:T(8,128)(2,1)S(1)} %collective-permute-done.refs_3_) | copy-start | bytes 3145732
  14.9 21.5 %collective-permute-start.1 = (bf16[2,2048,128]{2,1,0:T(8,128)(2,1)}, bf16[2,2048,128]{2,1,0:T(8,128)(2,1)}, u32[]{:S(2)}, u32[]{:S(2)}) collective-permute-start(bf16[2,2048,128]{2,1,0:T(8,128)(2,1)} %broadcast_select_fusion), channel_id=1, source_target_pairs={{0,8},{16,24},{32,40},{48,56},{64,72},{80,88},{96,104},{112,120},{... | collective-permute-start | bytes 3145736 | tf_op jit(solution)/shard_map/ppermute | solution.py:282
  51.2 1.2 copy-start
  67.3 20.2 %collective-permute-start.5 = (bf16[64,1536]{1,0:T(8,128)(2,1)}, bf16[64,1536]{1,0:T(8,128)(2,1)S(1)}, u32[]{:S(2)}, u32[]{:S(2)}) collective-permute-start(bf16[64,1536]{1,0:T(8,128)(2,1)} %get-tuple-element.36), channel_id=1, source_target_pairs={{0,4},{1,5},{2,6},{3,7},{4,0},{5,1},{6,2},{7,3},{8,12},{9,13},{10,... | collective-permute-start | bytes 589832 | tf_op jit(solution)/shard_map/ppermute | solution.py:287
  67.6 22.1 %collective-permute-start.6 = (bf16[64,1536]{1,0:T(8,128)(2,1)}, bf16[64,1536]{1,0:T(8,128)(2,1)S(1)}, u32[]{:S(2)}, u32[]{:S(2)}) collective-permute-start(bf16[64,1536]{1,0:T(8,128)(2,1)} %get-tuple-element.37), channel_id=1, source_target_pairs={{0,5},{1,4},{2,7},{3,6},{4,1},{5,0},{6,3},{7,2},{8,13},{9,12},{10,... | collective-permute-start | bytes 589832 | tf_op jit(solution)/shard_map/ppermute | solution.py:287
  87.5 13.7 %copy-start.2 = (bf16[64,1536]{1,0:T(8,128)(2,1)}, bf16[64,1536]{1,0:T(8,128)(2,1)S(1)}, u32[]{:S(2)}) copy-start(bf16[64,1536]{1,0:T(8,128)(2,1)S(1)} %collective-permute-done.5.refs_4_) | copy-start | bytes 589828
  89.7 11.5 %copy-start.3 = (bf16[64,1536]{1,0:T(8,128)(2,1)}, bf16[64,1536]{1,0:T(8,128)(2,1)S(1)}, u32[]{:S(2)}) copy-start(bf16[64,1536]{1,0:T(8,128)(2,1)S(1)} %collective-permute-done.6.refs_5_) | copy-start | bytes 589828
  89.7 6.8 %collective-permute-start.9 = (f32[2,2048,128]{2,1,0:T(8,128)}, f32[2,2048,128]{2,1,0:T(8,128)S(1)}, u32[]{:S(2)}, u32[]{:S(2)}) collective-permute-start(f32[2,2048,128]{2,1,0:T(8,128)} %get-tuple-element.47), channel_id=1, source_target_pairs={{8,0},{24,16},{40,32},{56,48},{72,64},{88,80},{104,96},{120,112},{... | collective-permute-start | bytes 6291464 | tf_op jit(solution)/shard_map/ppermute | solution.py:282
  92.7 11.4 %collective-permute-start.2 = (bf16[64,1536]{1,0:T(8,128)(2,1)}, bf16[64,1536]{1,0:T(8,128)(2,1)S(1)}, u32[]{:S(2)}, u32[]{:S(2)}) collective-permute-start(bf16[64,1536]{1,0:T(8,128)(2,1)} %get-tuple-element.32), channel_id=1, source_target_pairs={{0,1},{1,0},{2,3},{3,2},{4,5},{5,4},{6,7},{7,6},{8,9},{9,8},{10,11... | collective-permute-start | bytes 589832 | tf_op jit(solution)/shard_map/ppermute | solution.py:287
  93.6 12.7 %collective-permute-start.3 = (bf16[64,1536]{1,0:T(8,128)(2,1)}, bf16[64,1536]{1,0:T(8,128)(2,1)S(1)}, u32[]{:S(2)}, u32[]{:S(2)}) collective-permute-start(bf16[64,1536]{1,0:T(8,128)(2,1)} %get-tuple-element.33), channel_id=1, source_target_pairs={{0,2},{1,3},{2,0},{3,1},{4,6},{5,7},{6,4},{7,5},{8,10},{9,11},{10,... | collective-permute-start | bytes 589832 | tf_op jit(solution)/shard_map/ppermute | solution.py:287
  93.9 22.3 %collective-permute-start.4 = (bf16[64,1536]{1,0:T(8,128)(2,1)}, bf16[64,1536]{1,0:T(8,128)(2,1)S(1)}, u32[]{:S(2)}, u32[]{:S(2)}) collective-permute-start(bf16[64,1536]{1,0:T(8,128)(2,1)} %get-tuple-element.34), channel_id=1, source_target_pairs={{0,3},{1,2},{2,1},{3,0},{4,7},{5,6},{6,5},{7,4},{8,11},{9,10},{10,... | collective-permute-start | bytes 589832 | tf_op jit(solution)/shard_map/ppermute | solution.py:287
  96.3 20.6 %collective-permute-start.7 = (bf16[64,1536]{1,0:T(8,128)(2,1)}, bf16[64,1536]{1,0:T(8,128)(2,1)S(1)}, u32[]{:S(2)}, u32[]{:S(2)}) collective-permute-start(bf16[64,1536]{1,0:T(8,128)(2,1)} %get-tuple-element.40), channel_id=1, source_target_pairs={{0,6},{1,7},{2,4},{3,5},{4,2},{5,3},{6,0},{7,1},{8,14},{9,15},{10,... | collective-permute-start | bytes 589832 | tf_op jit(solution)/shard_map/ppermute | solution.py:287
  96.6 21.0 %collective-permute-start.8 = (bf16[64,1536]{1,0:T(8,128)(2,1)}, bf16[64,1536]{1,0:T(8,128)(2,1)S(1)}, u32[]{:S(2)}, u32[]{:S(2)}) collective-permute-start(bf16[64,1536]{1,0:T(8,128)(2,1)} %get-tuple-element.41), channel_id=1, source_target_pairs={{0,7},{1,6},{2,5},{3,4},{4,3},{5,2},{6,1},{7,0},{8,15},{9,14},{10,... | collective-permute-start | bytes 589832 | tf_op jit(solution)/shard_map/ppermute | solution.py:287
  104.1 1.6 %copy-start.4 = (bf16[64,1536]{1,0:T(8,128)(2,1)}, bf16[64,1536]{1,0:T(8,128)(2,1)S(1)}, u32[]{:S(2)}) copy-start(bf16[64,1536]{1,0:T(8,128)(2,1)S(1)} %collective-permute-done.2.refs_1_) | copy-start | bytes 589828
  104.1 16.9 %collective-permute-start.10 = (bf16[2,2048,128]{2,1,0:T(8,128)(2,1)S(1)}, bf16[2,2048,128]{2,1,0:T(8,128)(2,1)}, u32[]{:S(2)}, u32[]{:S(2)}) collective-permute-start(bf16[2,2048,128]{2,1,0:T(8,128)(2,1)S(1)} %get-tuple-element.48), channel_id=1, source_target_pairs={{16,0},{48,32},{80,64},{112,96},{144,128},{176,160},{208,192},{240... | collective-permute-start | bytes 3145736 | tf_op jit(solution)/shard_map/ppermute | solution.py:282
  106.3 0.7 copy-start.5
  116.2 0.7 copy-start.6
  116.9 0.7 copy-start.7
  117.6 0.7 copy-start.8

commit v3 on v2

--- a/solution.py
+++ b/solution.py
@@ -42,9 +42,7 @@
     return pl.ds(pl.multiple_of(part * width, HD), width)
 
 
-def pack_kernel(q, k, v, g, pk, pv, prefix, out):
-    prefix[0] = pk[...]
-    prefix[1] = pv[...]
+def pack_kernel(q, k, v, g, out):
     for m in range(PARTS):
         wide, thin = slice(m * WIDE, (m + 1) * WIDE), slice(m * HD, (m + 1) * HD)
         out[m, :, :WIDE] = q[:, wide]
@@ -53,39 +51,38 @@
         out[m, :, 2 * WIDE + HD :] = v[:, thin]
 
 
-def pack(q, k, v, g, pk, pv):
+def pack(q, k, v, g):
     vmem = pl.BlockSpec(memory_space=pltpu.VMEM)
     return pl.pallas_call(
         pack_kernel,
-        in_specs=[vmem] * 6,
-        out_specs=[vmem] * 2,
-        out_shape=[
-            jax.ShapeDtypeStruct((2, PREFIX, HD), BF16),
-            jax.ShapeDtypeStruct((PARTS, ROWS, SEND), BF16),
-        ],
+        in_specs=[vmem] * 4,
+        out_specs=vmem,
+        out_shape=jax.ShapeDtypeStruct((PARTS, ROWS, SEND), BF16),
         name="pack",
-    )(q, k, v, g, pk, pv)
+    )(q, k, v, g)
 
 
 def unpack_kernel(ids, *refs):
-    bufs, (o, dq, dk, dv) = refs[:PARTS], refs[PARTS:]
+    bufs, (near, _, o, dq, dk, dv) = refs[:QUAD], refs[QUAD:]
     me = ids[1]
-    for p in range(PARTS):
-        cols = head_columns(me ^ p, WIDE)
-        o[:, cols] = bufs[p][:, :WIDE]
-        dq[:, cols] = bufs[p][:, WIDE : 2 * WIDE]
-        cols = head_columns(me ^ p, HD)
-        dk[:, cols] = bufs[p][:, 2 * WIDE : 2 * WIDE + HD]
-        dv[:, cols] = bufs[p][:, 2 * WIDE + HD :]
-
-
-def unpack(ids, bufs):
+    parts = [((me ^ QUAD) ^ p, bufs[p]) for p in range(QUAD)]
+    parts += [((me & QUAD) + n, near.at[n]) for n in range(QUAD)]
+    for m, part in parts:
+        cols = head_columns(m, WIDE)
+        o[:, cols] = part[:, :WIDE]
+        dq[:, cols] = part[:, WIDE : 2 * WIDE]
+        cols = head_columns(m, HD)
+        dk[:, cols] = part[:, 2 * WIDE : 2 * WIDE + HD]
+        dv[:, cols] = part[:, 2 * WIDE + HD :]
+
+
+def unpack(ids, *bufs):
     vmem = pl.BlockSpec(memory_space=pltpu.VMEM)
     wide = jax.ShapeDtypeStruct((ROWS, PARTS * WIDE), BF16)
     thin = jax.ShapeDtypeStruct((ROWS, PARTS * HD), BF16)
     return pl.pallas_call(
         unpack_kernel,
-        in_specs=[pl.BlockSpec(memory_space=pltpu.SMEM)] + [vmem] * PARTS,
+        in_specs=[pl.BlockSpec(memory_space=pltpu.SMEM)] + [vmem] * (QUAD + 1) + [ANY],
         out_specs=[vmem] * 4,
         out_shape=[wide, wide, thin, thin],
         cost_estimate=pl.CostEstimate(flops=1 << 36, bytes_accessed=4 << 20, transcendentals=0),
@@ -94,12 +91,13 @@
 
 
 def attend_kernel(far, chained, ids, prompt_of, lengths, *refs):
-    bufs, refs = refs[0], refs[1:]
+    rows_in, refs = refs[0], refs[1:]
     pk, pv, far_prefix, near_prefix = refs[:4]
     refs = refs[4 + 2 * chained :]
-    outs, refs = refs[:QUAD], refs[QUAD:]
+    sent = QUAD if far else 1
+    outs, refs = refs[:sent], refs[sent:]
     own_ref, lead_ref, q_ref, g_ref, k_own, v_own, e_ref, w_ref, d_ref = refs[:9]
-    kt_ref, vt_ref, move_ref, pre_ref, acc_ref, pre_sem, acc_sem = refs[9:]
+    kt_ref, vt_ref, move_ref, pre_ref, acc_ref, bufs, out_ref, pre_sem, acc_sem, row_sem, out_sem = refs[9:]
     dp_at, part = ids[0], ids[1]
     slot = (part >> 2) ^ far
     length = lengths[slot]
@@ -107,6 +105,8 @@
     place = dp_at & 3
     source = jnp.where((role == 0) | (place == 0), 0, jnp.where(place == 2, 1, 2))
     places = [((part ^ n) & 3) * ROWS for n in range(QUAD)]
+    rows_load = pltpu.make_async_copy(rows_in.at[pl.ds(slot * QUAD, QUAD)], bufs, row_sem)
+    rows_load.start()
 
     def token_rows(n):
         return pl.ds(pl.multiple_of(places[n], ROWS), ROWS)
@@ -129,6 +129,7 @@
     def value_rows(i):
         return v_own[...] if i == STEPS - 1 else pre_ref[1, rows[i], :]
 
+    rows_load.wait()
     zero = jnp.zeros((), BF16)
     row = lax.broadcasted_iota(jnp.int32, (ROWS, HD), 0)
     for n in range(QUAD):
@@ -167,7 +168,8 @@
     def give(column, x):
         move_ref[...] = x
         for n in range(QUAD):
-            outs[n][:, column * HD : (column + 1) * HD] = move_ref[token_rows(n), :]
+            at = token_rows(n) if far else pl.ds(n * ROWS, ROWS)
+            out_ref[n, :, column * HD : (column + 1) * HD] = move_ref[at, :]
 
     def weigh(h, i):
         w_ref[rows[i], cols[h]] = (e_ref[rows[i], cols[h]] * scales[h][i]).astype(BF16)
@@ -185,6 +187,17 @@
 
     def d_queries(h):
         give(GROUP + h, (nn(kt_ref[...], d_ref[:, cols[h]]) * SCALE).astype(BF16).T)
+
+    early = slice(0, (GROUP - 2) * CLEN)
+    late = slice((GROUP - 2) * CLEN, COLS)
+
+    def sums_over(i, of):
+        dk = nn(d_ref[rows[i], of], q_ref[of, :])
+        dv = nn(w_ref[rows[i], of], g_ref[of, :])
+        return dk, dv
+
+    def early_sums(i):
+        acc_ref[0, rows[i], :], acc_ref[1, rows[i], :] = sums_over(i, early)
 
     for n in range(GROUP + 2):
         for i in order:
@@ -200,6 +213,8 @@
                 weigh(n - 1, i)
             if n >= 2:
                 d_scores(n - 2, i)
+            if n == GROUP:
+                early_sums(i)
         if n < GROUP:
             normalise(n)
         if 1 <= n <= GROUP:
@@ -211,12 +226,19 @@
         piece = pl.ds(n * PIECE, PIECE)
         return pltpu.make_async_copy(acc_ref.at[:, piece, :], target.at[:, piece, :], acc_sem.at[n])
 
+    pieces = [out_ref.at[n] for n in range(QUAD)] if far else [out_ref]
+    results = [
+        pltpu.make_async_copy(pieces[n], outs[n], out_sem.at[n]) for n in range(sent)
+    ]
     for i in order:
-        dk = nn(d_ref[rows[i], :], q_ref[...]) * SCALE
-        dv = nn(w_ref[rows[i], :], g_ref[...])
+        dk, dv = sums_over(i, late)
+        dk = (acc_ref[0, rows[i], :] + dk) * SCALE
+        dv = acc_ref[1, rows[i], :] + dv
         if i == STEPS - 1:
             give(2 * GROUP, dk.astype(BF16))
             give(2 * GROUP + 1, dv.astype(BF16))
+            for copy in results:
+                copy.start()
             continue
         acc_ref[0, rows[i], :] = dk
         acc_ref[1, rows[i], :] = dv
@@ -230,22 +252,23 @@
             def _():
                 store_copy(i // 2, lead_ref).start()
 
+    for copy in results:
+        copy.wait()
     for n in range(4):
         store_copy(n, own_ref).wait()
 
 
 def attend(name, far, scalars, rows, prefix, leads, chain=()):
-    whole = pl.BlockSpec((ROWS, SEND), lambda n, *_: (0, 0))
-    quad = pl.BlockSpec((QUAD, ROWS, SEND), lambda n, ids, *_: ((ids[1] >> 2) ^ far, 0, 0))
     args = [rows, *prefix, *leads, *chain]
+    sent = [(ROWS, SEND)] * QUAD if far else [(QUAD, ROWS, SEND)]
     grads = jax.ShapeDtypeStruct((2, PREFIX, HD), F32)
     return pl.pallas_call(
         functools.partial(attend_kernel, far, len(chain) > 0),
         grid_spec=pltpu.PrefetchScalarGridSpec(
             num_scalar_prefetch=3,
             grid=(1,),
-            in_specs=[quad] + [ANY] * (4 + len(chain)),
-            out_specs=[whole] * QUAD + [ANY] * 2,
+            in_specs=[ANY] * (5 + len(chain)),
+            out_specs=[ANY] * (len(sent) + 2),
             scratch_shapes=[
                 pltpu.VMEM((COLS, HD), BF16),
                 pltpu.VMEM((COLS, HD), BF16),
@@ -258,14 +281,18 @@
                 pltpu.VMEM((HD, KEYS), BF16),
                 pltpu.VMEM((CLEN, HD), BF16),
                 pltpu.VMEM((2, PREFIX, HD), BF16),
-                pltpu.VMEM((2, PREFIX, HD), F32),
+                pltpu.VMEM((2, KEYS, HD), F32),
+                pltpu.VMEM((QUAD, ROWS, SEND), BF16),
+                pltpu.VMEM((QUAD, ROWS, SEND), BF16),
                 pltpu.SemaphoreType.DMA((2,)),
                 pltpu.SemaphoreType.DMA((4,)),
+                pltpu.SemaphoreType.DMA(()),
+                pltpu.SemaphoreType.DMA((QUAD,)),
             ],
         ),
-        out_shape=[jax.ShapeDtypeStruct((ROWS, SEND), BF16)] * QUAD + [grads] * 2,
-        input_output_aliases={3 + len(args) - 2 + n: QUAD + n for n in range(len(chain))},
-        compiler_params=pltpu.CompilerParams(vmem_limit_bytes=62 * 1024 * 1024),
+        out_shape=[jax.ShapeDtypeStruct(x, BF16) for x in sent] + [grads] * 2,
+        input_output_aliases={3 + len(args) - 2 + n: len(sent) + n for n in range(len(chain))},
+        compiler_params=pltpu.CompilerParams(vmem_limit_bytes=63 * 1024 * 1024),
         cost_estimate=pl.CostEstimate(flops=1 << 20, bytes_accessed=1 << 16, transcendentals=0),
         name=name,
     )(*scalars, *args)
@@ -286,27 +313,34 @@
     def swap(x, p):
         return lax.ppermute(x, "mp", [(i, i ^ p) for i in range(PARTS)])
 
-    prefix, rows = pack(queries, keys, values, cotangent, pk, pv)
+    rows = pack(queries, keys, values, cotangent)
+    rows, *prefix = lax.optimization_barrier((rows, prefix_keys, prefix_values))
+    prefix = jnp.concatenate(prefix, 0)
     leader = me % REACH == 0
     far = send(prefix, (0, 2))
     near = send(jnp.where(leader, prefix, far), (0, 1), (2, 3))
     leads = (far, near)
     rows = lax.all_to_all(rows, "mp", split_axis=0, concat_axis=0, tiled=True)
-    *back_far, own_grads, lead_grads = attend("far", 1, scalars, rows, (pk, pv), leads)
-    *back_near, own_grads, lead_grads = attend(
+    *back, own_grads, lead_grads = attend("far", 1, scalars, rows, (pk, pv), leads)
+    back_near, own_grads, lead_grads = attend(
         "near", 0, scalars, rows, (pk, pv), leads, (own_grads, lead_grads)
     )
-    back = back_near + back_far
-    back = [back[0]] + [swap(back[p], p) for p in range(1, PARTS)]
-
-    lead_grads, *back[4:6] = lax.optimization_barrier((lead_grads, *back[4:6]))
-    near_sum = lead_grads + send(lead_grads, (1, 0), (3, 2))
-    far_grads = send(near_sum.astype(BF16), (2, 0))
-    base = own_grads + jnp.where(leader, near_sum, 0.0)
+    back = [swap(x, QUAD + n) for n, x in enumerate(back)]
+    quads = [list(range(n, n + QUAD)) for n in range(0, PARTS, QUAD)]
+    back_near = lax.all_to_all(
+        back_near, "mp", split_axis=0, concat_axis=0, axis_index_groups=quads, tiled=True
+    )
+
+    lead_grads, *back[:2] = lax.optimization_barrier((lead_grads, *back[:2]))
+    near_grads = send(lead_grads, (1, 0), (3, 2))
+    near_sum = (lead_grads + near_grads).astype(BF16)
+    far_grads = send(near_sum, (2, 0))
+    near_sum, near_grads = lax.optimization_barrier((near_sum, near_grads))
+    base = own_grads + jnp.where(leader, lead_grads + near_grads, 0.0)
     d_keys, d_values = (
         (base[n] + far_grads[n].astype(F32)).astype(BF16)[None] for n in range(2)
     )
-    outs = unpack(ids, back)
+    outs = unpack(ids, *back, back_near, base)
     return (*outs, d_keys, d_values)
 
 

time: 124 us -> 123 us (level)
  the two profiles are of different devices: /device:TPU:1 before, /device:TPU:61 now
where the time goes in v3:
time: 123 us
  waiting for transfers between devices  51 us (41%)
  Pallas kernels  32.3 us (26%)
  starting transfers between devices  29.4 us (24%)
  other arithmetic  6.56 us (5%)
  local copies, waits for them, and re-layouts  2.67 us (2%)
    pallas_call x2, Pallas kernels, attend(): pl.pallas_call(functools.partial(attend_kernel, far, len(chain) > 0), gri...  26.8 us
    ppermute x4, waiting for transfers between devices, send(): lax.ppermute(x, 'dp', [(REACH * n + a, REACH * n + b) for n in range(grou...  19 us
    ppermute x4, waiting for transfers between devices, swap(): return lax.ppermute(x, 'mp', [(i, i ^ p) for i in range(PARTS)])  16.9 us
    all_to_all x1, waiting for transfers between devices, local(): rows = lax.all_to_all(rows, 'mp', split_axis=0, concat_axis=0, tiled=True)  13.3 us
    ppermute x4, starting transfers between devices, swap(): return lax.ppermute(x, 'mp', [(i, i ^ p) for i in range(PARTS)])  8.55 us
    all_to_all x1, starting transfers between devices, local(): rows = lax.all_to_all(rows, 'mp', split_axis=0, concat_axis=0, tiled=True)  8.14 us
    all_to_all x1, starting transfers between devices, local(): lax.all_to_all(back_near, 'mp', split_axis=0, concat_axis=0, axis_index_g...  6.58 us
    ppermute x4, starting transfers between devices, send(): lax.ppermute(x, 'dp', [(REACH * n + a, REACH * n + b) for n in range(grou...  6.18 us
  transfers between devices with their start and end apart: 10, of which 6 were waited for; matrix products, arithmetic and copies ran while one was open for 5% of the time, Pallas kernels for 13%

profile of v3, /device:TPU:61, one launch (start us, length us, event | category | flops | bytes accessed | tf_op | source)
XLA Modules:
  0.0 122.7 jit_solution(12354893423521665263)
XLA Ops:
  0.6 2.7 %pack.1 = bf16[8,64,1536]{2,1,0:T(8,128)(2,1)} custom-call(bf16[64,5120]{1,0:T(8,128)(2,1)} %q.1, bf16[64,1024]{1,0:T(8,128)(2,1)} %k.1, bf16[64,1024]{1,0:T(8,128)(2,1)} %v.1, bf16[64,5120]{1,0:T(8,128)(2,1)} %g.1), custom_call_target="tpu_custom_call" | custom-call | tf_op jit(solution)/shard_map/pack/pallas_call | solution.py:56
  3.3 0.0 copy-start.4
  3.3 0.0 copy-start.5
  3.3 8.1 %all-to-all-start = ((bf16[8,64,1536]{2,1,0:T(8,128)(2,1)}), bf16[8,64,1536]{2,1,0:T(8,128)(2,1)}, u32[]{:S(2)}, u32[]{:S(2)}) async-start(bf16[8,64,1536]{2,1,0:T(8,128)(2,1)} %pack.1), calls=%async_computation | async-start | bytes 3145728 | tf_op jit(solution)/shard_map/all_to_all | solution.py:323
  11.5 0.0 copy-done.4
  11.5 0.8 constant_dynamic-update-slice_fusion.1
  12.3 0.0 copy-done.5
  12.3 0.8 constant_dynamic-update-slice_fusion
  13.2 0.7 collective-permute-start
  13.9 0.0 collective-permute-done.refs_3_
  13.9 0.0 copy-start.1
  13.9 1.0 copy-done.1
  14.9 0.1 broadcast_select_fusion
  15.0 1.3 %collective-permute-start.1 = (bf16[2,2048,128]{2,1,0:T(8,128)(2,1)S(1)}, bf16[2,2048,128]{2,1,0:T(8,128)(2,1)}, u32[]{:S(2)}, u32[]{:S(2)}) collective-permute-start(bf16[2,2048,128]{2,1,0:T(8,128)(2,1)S(1)} %broadcast_select_fusion), channel_id=1, source_target_pairs={{0,8},{16,24},{32,40},{48,56},{64,72},{80,88},{96,104},{112,120},{... | collective-permute-start | bytes 3145736 | tf_op jit(solution)/shard_map/ppermute | solution.py:309
  16.3 0.7 pad_add_fusion.ids
  17.0 19.0 %collective-permute-done.1.refs_4_ = bf16[2,2048,128]{2,1,0:T(8,128)(2,1)} collective-permute-done((bf16[2,2048,128]{2,1,0:T(8,128)(2,1)S(1)}, bf16[2,2048,128]{2,1,0:T(8,128)(2,1)}, u32[]{:S(2)}, u32[]{:S(2)}) %collective-permute-start.1) | collective-permute-done | bytes 1048608 | tf_op jit(solution)/shard_map/ppermute | solution.py:309
  35.9 13.3 %all-to-all-done.refs_0_ = bf16[8,64,1536]{2,1,0:T(8,128)(2,1)} async-done(((bf16[8,64,1536]{2,1,0:T(8,128)(2,1)}), bf16[8,64,1536]{2,1,0:T(8,128)(2,1)}, u32[]{:S(2)}, u32[]{:S(2)}) %all-to-all-start) | async-done | bytes 1572896 | tf_op jit(solution)/shard_map/all_to_all | solution.py:323
  49.2 13.6 %far.1 = (bf16[64,1536]{1,0:T(8,128)(2,1)}, bf16[64,1536]{1,0:T(8,128)(2,1)}, bf16[64,1536]{1,0:T(8,128)(2,1)}, bf16[64,1536]{1,0:T(8,128)(2,1)}, f32[2,2048,128]{2,1,0:T(8,128)}, /*index=5*/f32[2,2048,128]{2,1,0:T(8,128)}) custom-call(s32[2]{0:T(128)} %pad_add_fusion.ids, s32[2]{0:T(128)} %prompt_of.3, s32[2]{0:T(128)} %lengths.3, ...), custom_call_target="tpu_custom_call" | custom-call | flops 1048576 | bytes 65536 | tf_op jit(solution)/shard_map/far/pallas_call | solution.py:265
  62.8 0.4 collective-permute-start.2
  63.2 4.7 %collective-permute-start.3 = (bf16[64,1536]{1,0:T(8,128)(2,1)}, bf16[64,1536]{1,0:T(8,128)(2,1)S(1)}, u32[]{:S(2)}, u32[]{:S(2)}) collective-permute-start(bf16[64,1536]{1,0:T(8,128)(2,1)} %get-tuple-element.33), channel_id=1, source_target_pairs={{0,5},{1,4},{2,7},{3,6},{4,1},{5,0},{6,3},{7,2},{8,13},{9,12},{10,... | collective-permute-start | bytes 589832 | tf_op jit(solution)/shard_map/ppermute | solution.py:314
  67.9 13.2 %near.1 = (bf16[4,64,1536]{2,1,0:T(8,128)(2,1)}, f32[2,2048,128]{2,1,0:T(8,128)}, f32[2,2048,128]{2,1,0:T(8,128)}) custom-call(s32[2]{0:T(128)} %pad_add_fusion.ids, s32[2]{0:T(128)} %prompt_of.3, s32[2]{0:T(128)} %lengths.3, bf16[8,64,1536]{2,1,0:T(8,128)(2,1)} %all-to-all-done.refs_0_, ...), custom_call_target="tpu_custom_call", output_to_operand_aliasing={{1}: (8, {}), {2}: (9, {})} | custom-call | flops 1048576 | bytes 65536 | tf_op jit(solution)/shard_map/near/pallas_call | solution.py:265
  81.1 0.0 collective-permute-done.2.refs_0_
  81.1 0.0 copy-start.6
  81.1 3.1 %collective-permute-done.3.refs_1_ = bf16[64,1536]{1,0:T(8,128)(2,1)S(1)} collective-permute-done((bf16[64,1536]{1,0:T(8,128)(2,1)}, bf16[64,1536]{1,0:T(8,128)(2,1)S(1)}, u32[]{:S(2)}, u32[]{:S(2)}) %collective-permute-start.3) | collective-permute-done | bytes 196640 | tf_op jit(solution)/shard_map/ppermute | solution.py:314
  84.2 0.0 copy-start.7
  84.2 2.5 %collective-permute-start.6 = (f32[2,2048,128]{2,1,0:T(8,128)}, f32[2,2048,128]{2,1,0:T(8,128)S(1)}, u32[]{:S(2)}, u32[]{:S(2)}) collective-permute-start(f32[2,2048,128]{2,1,0:T(8,128)} %get-tuple-element.40), channel_id=1, source_target_pairs={{8,0},{24,16},{40,32},{56,48},{72,64},{88,80},{104,96},{120,112},{... | collective-permute-start | bytes 6291464 | tf_op jit(solution)/shard_map/ppermute | solution.py:309
  86.8 6.6 %all-to-all-start.1 = ((bf16[4,64,1536]{2,1,0:T(8,128)(2,1)}), bf16[4,64,1536]{2,1,0:T(8,128)(2,1)}, u32[]{:S(2)}, u32[]{:S(2)}) async-start(bf16[4,64,1536]{2,1,0:T(8,128)(2,1)} %get-tuple-element.38), calls=%async_computation.1 | async-start | bytes 1572864 | tf_op jit(solution)/shard_map/all_to_all | solution.py:330
  93.3 0.3 collective-permute-start.4
  93.6 0.0 copy-start
  93.6 0.0 copy-start.2
  93.7 3.1 %collective-permute-start.5 = (bf16[64,1536]{1,0:T(8,128)(2,1)}, bf16[64,1536]{1,0:T(8,128)(2,1)}, u32[]{:S(2)}, u32[]{:S(2)}) collective-permute-start(bf16[64,1536]{1,0:T(8,128)(2,1)} %get-tuple-element.37), channel_id=1, source_target_pairs={{0,7},{1,6},{2,5},{3,4},{4,3},{5,2},{6,1},{7,0},{8,15},{9,14},{10,... | collective-permute-start | bytes 589832 | tf_op jit(solution)/shard_map/ppermute | solution.py:314
  96.8 0.0 collective-permute-done.6
  96.8 1.8 %add_convert_fusion = bf16[2,2048,128]{2,1,0:T(8,128)(2,1)S(1)} fusion(f32[2,2048,128]{2,1,0:T(8,128)} %get-tuple-element.40, f32[2,2048,128]{2,1,0:T(8,128)S(1)} %collective-permute-done.6), kind=kLoop, calls=%fused_computation.1 | loop fusion | flops 1048576 | bytes 5242880 | tf_op jit(solution)/shard_map/convert_element_type | solution.py:336
  98.6 0.0 copy-done.6
  98.6 0.0 copy-done.7
  98.6 1.7 %collective-permute-start.7 = (bf16[2,2048,128]{2,1,0:T(8,128)(2,1)S(1)}, bf16[2,2048,128]{2,1,0:T(8,128)(2,1)}, u32[]{:S(2)}, u32[]{:S(2)}) collective-permute-start(bf16[2,2048,128]{2,1,0:T(8,128)(2,1)S(1)} %add_convert_fusion), channel_id=1, source_target_pairs={{16,0},{48,32},{80,64},{112,96},{144,128},{176,160},{208,192},{240... | collective-permute-start | bytes 3145736 | tf_op jit(solution)/shard_map/ppermute | solution.py:309
  100.3 0.0 copy-done
  100.3 0.0 copy-done.2
  100.3 1.6 %select_add_fusion.refs_5_ = f32[2,2048,128]{2,1,0:T(8,128)} fusion(f32[2,2048,128]{2,1,0:T(8,128)S(1)} %copy-done.2, f32[2,2048,128]{2,1,0:T(8,128)S(1)} %copy-done, f32[2,2048,128]{2,1,0:T(8,128)S(1)} %collective-permute-done.6, pred[]{:T(512)S(6)} %eq.5), kind=kLoop, calls=%fused_computation | loop fusion | flops 1572864 | bytes 8388609 | tf_op jit(solution)/shard_map/add | solution.py:339
  101.9 0.0 copy-start.3
  101.9 9.1 %collective-permute-done.4.refs_2_ = bf16[64,1536]{1,0:T(8,128)(2,1)} collective-permute-done((bf16[64,1536]{1,0:T(8,128)(2,1)}, bf16[64,1536]{1,0:T(8,128)(2,1)}, u32[]{:S(2)}, u32[]{:S(2)}) %collective-permute-start.4) | collective-permute-done | bytes 196640 | tf_op jit(solution)/shard_map/ppermute | solution.py:314
  111.0 4.7 %collective-permute-done.5.refs_3_ = bf16[64,1536]{1,0:T(8,128)(2,1)} collective-permute-done((bf16[64,1536]{1,0:T(8,128)(2,1)}, bf16[64,1536]{1,0:T(8,128)(2,1)}, u32[]{:S(2)}, u32[]{:S(2)}) %collective-permute-start.5) | collective-permute-done | bytes 196640 | tf_op jit(solution)/shard_map/ppermute | solution.py:314
  115.7 1.8 %all-to-all-done.1.refs_4_ = bf16[4,64,1536]{2,1,0:T(8,128)(2,1)} async-done(((bf16[4,64,1536]{2,1,0:T(8,128)(2,1)}), bf16[4,64,1536]{2,1,0:T(8,128)(2,1)}, u32[]{:S(2)}, u32[]{:S(2)}) %all-to-all-start.1) | async-done | bytes 786464 | tf_op jit(solution)/shard_map/all_to_all | solution.py:330
  117.5 2.8 %unpack.1 = (bf16[64,5120]{1,0:T(8,128)(2,1)}, bf16[64,5120]{1,0:T(8,128)(2,1)}, bf16[64,1024]{1,0:T(8,128)(2,1)}, bf16[64,1024]{1,0:T(8,128)(2,1)}) custom-call(s32[2]{0:T(128)} %pad_add_fusion.ids, bf16[64,1536]{1,0:T(8,128)(2,1)} %copy-done.6, bf16[64,1536]{1,0:T(8,128)(2,1)} %copy-done.7, bf16[64,1536]{1,0:T(8,128)(2,1)} %collective-permute-done.4.refs_2_, ...), custom_call_target="tpu_custom_call" | custom-call | flops 68719476736 | bytes 4194304 | tf_op jit(solution)/shard_map/unpack/pallas_call | solution.py:83
  120.3 0.0 collective-permute-done.7
  120.3 0.0 copy-done.3
  120.3 2.4 %fusion = (bf16[1,2048,128]{2,1,0:T(8,128)(2,1)}, bf16[1,2048,128]{2,1,0:T(8,128)(2,1)}) fusion(f32[2,2048,128]{2,1,0:T(8,128)S(1)} %copy-done.3, bf16[2,2048,128]{2,1,0:T(8,128)(2,1)} %collective-permute-done.7), kind=kLoop, calls=%fused_computation.3 | loop fusion | flops 1572864 | bytes 4194304 | tf_op jit(solution)/shard_map/convert_element_type | solution.py:341
Async XLA Ops:
  3.3 8.1 %copy-start.4 = (bf16[1,2048,128]{2,1,0:T(8,128)(2,1)S(1)}, bf16[1,2048,128]{2,1,0:T(8,128)(2,1)}, u32[]{:S(2)}) copy-start(bf16[1,2048,128]{2,1,0:T(8,128)(2,1)} %param.11) | copy-start | bytes 1572868
  3.3 9.0 %copy-start.5 = (bf16[1,2048,128]{2,1,0:T(8,128)(2,1)S(1)}, bf16[1,2048,128]{2,1,0:T(8,128)(2,1)}, u32[]{:S(2)}) copy-start(bf16[1,2048,128]{2,1,0:T(8,128)(2,1)} %param.12) | copy-start | bytes 1572868
  3.3 45.9 %all-to-all-start = ((bf16[8,64,1536]{2,1,0:T(8,128)(2,1)}), bf16[8,64,1536]{2,1,0:T(8,128)(2,1)}, u32[]{:S(2)}, u32[]{:S(2)}) async-start(bf16[8,64,1536]{2,1,0:T(8,128)(2,1)} %pack.1), calls=%async_computation | async-start | bytes 3145728 | tf_op jit(solution)/shard_map/all_to_all | solution.py:323
  13.2 0.7 collective-permute-start
  13.9 1.0 copy-start.1
  15.0 20.9 %collective-permute-start.1 = (bf16[2,2048,128]{2,1,0:T(8,128)(2,1)S(1)}, bf16[2,2048,128]{2,1,0:T(8,128)(2,1)}, u32[]{:S(2)}, u32[]{:S(2)}) collective-permute-start(bf16[2,2048,128]{2,1,0:T(8,128)(2,1)S(1)} %broadcast_select_fusion), channel_id=1, source_target_pairs={{0,8},{16,24},{32,40},{48,56},{64,72},{80,88},{96,104},{112,120},{... | collective-permute-start | bytes 3145736 | tf_op jit(solution)/shard_map/ppermute | solution.py:309
  62.8 18.3 %collective-permute-start.2 = (bf16[64,1536]{1,0:T(8,128)(2,1)}, bf16[64,1536]{1,0:T(8,128)(2,1)S(1)}, u32[]{:S(2)}, u32[]{:S(2)}) collective-permute-start(bf16[64,1536]{1,0:T(8,128)(2,1)} %get-tuple-element.32), channel_id=1, source_target_pairs={{0,4},{1,5},{2,6},{3,7},{4,0},{5,1},{6,2},{7,3},{8,12},{9,13},{10,... | collective-permute-start | bytes 589832 | tf_op jit(solution)/shard_map/ppermute | solution.py:314
  63.2 21.0 %collective-permute-start.3 = (bf16[64,1536]{1,0:T(8,128)(2,1)}, bf16[64,1536]{1,0:T(8,128)(2,1)S(1)}, u32[]{:S(2)}, u32[]{:S(2)}) collective-permute-start(bf16[64,1536]{1,0:T(8,128)(2,1)} %get-tuple-element.33), channel_id=1, source_target_pairs={{0,5},{1,4},{2,7},{3,6},{4,1},{5,0},{6,3},{7,2},{8,13},{9,12},{10,... | collective-permute-start | bytes 589832 | tf_op jit(solution)/shard_map/ppermute | solution.py:314
  81.1 17.5 %copy-start.6 = (bf16[64,1536]{1,0:T(8,128)(2,1)}, bf16[64,1536]{1,0:T(8,128)(2,1)S(1)}, u32[]{:S(2)}) copy-start(bf16[64,1536]{1,0:T(8,128)(2,1)S(1)} %collective-permute-done.2.refs_0_) | copy-start | bytes 589828
  84.2 14.4 %copy-start.7 = (bf16[64,1536]{1,0:T(8,128)(2,1)}, bf16[64,1536]{1,0:T(8,128)(2,1)S(1)}, u32[]{:S(2)}) copy-start(bf16[64,1536]{1,0:T(8,128)(2,1)S(1)} %collective-permute-done.3.refs_1_) | copy-start | bytes 589828
  84.2 12.5 %collective-permute-start.6 = (f32[2,2048,128]{2,1,0:T(8,128)}, f32[2,2048,128]{2,1,0:T(8,128)S(1)}, u32[]{:S(2)}, u32[]{:S(2)}) collective-permute-start(f32[2,2048,128]{2,1,0:T(8,128)} %get-tuple-element.40), channel_id=1, source_target_pairs={{8,0},{24,16},{40,32},{56,48},{72,64},{88,80},{104,96},{120,112},{... | collective-permute-start | bytes 6291464 | tf_op jit(solution)/shard_map/ppermute | solution.py:309
  86.8 30.8 %all-to-all-start.1 = ((bf16[4,64,1536]{2,1,0:T(8,128)(2,1)}), bf16[4,64,1536]{2,1,0:T(8,128)(2,1)}, u32[]{:S(2)}, u32[]{:S(2)}) async-start(bf16[4,64,1536]{2,1,0:T(8,128)(2,1)} %get-tuple-element.38), calls=%async_computation.1 | async-start | bytes 1572864 | tf_op jit(solution)/shard_map/all_to_all | solution.py:330
  93.3 17.7 %collective-permute-start.4 = (bf16[64,1536]{1,0:T(8,128)(2,1)}, bf16[64,1536]{1,0:T(8,128)(2,1)}, u32[]{:S(2)}, u32[]{:S(2)}) collective-permute-start(bf16[64,1536]{1,0:T(8,128)(2,1)} %get-tuple-element.36), channel_id=1, source_target_pairs={{0,6},{1,7},{2,4},{3,5},{4,2},{5,3},{6,0},{7,1},{8,14},{9,15},{10,... | collective-permute-start | bytes 589832 | tf_op jit(solution)/shard_map/ppermute | solution.py:314
  93.6 6.6 %copy-start = (f32[2,2048,128]{2,1,0:T(8,128)S(1)}, f32[2,2048,128]{2,1,0:T(8,128)}, u32[]{:S(2)}) copy-start(f32[2,2048,128]{2,1,0:T(8,128)} %get-tuple-element.40) | copy-start | bytes 6291460
  93.6 6.6 %copy-start.2 = (f32[2,2048,128]{2,1,0:T(8,128)S(1)}, f32[2,2048,128]{2,1,0:T(8,128)}, u32[]{:S(2)}) copy-start(f32[2,2048,128]{2,1,0:T(8,128)} %get-tuple-element.39) | copy-start | bytes 6291460
  93.7 22.0 %collective-permute-start.5 = (bf16[64,1536]{1,0:T(8,128)(2,1)}, bf16[64,1536]{1,0:T(8,128)(2,1)}, u32[]{:S(2)}, u32[]{:S(2)}) collective-permute-start(bf16[64,1536]{1,0:T(8,128)(2,1)} %get-tuple-element.37), channel_id=1, source_target_pairs={{0,7},{1,6},{2,5},{3,4},{4,3},{5,2},{6,1},{7,0},{8,15},{9,14},{10,... | collective-permute-start | bytes 589832 | tf_op jit(solution)/shard_map/ppermute | solution.py:314
  98.6 21.7 %collective-permute-start.7 = (bf16[2,2048,128]{2,1,0:T(8,128)(2,1)S(1)}, bf16[2,2048,128]{2,1,0:T(8,128)(2,1)}, u32[]{:S(2)}, u32[]{:S(2)}) collective-permute-start(bf16[2,2048,128]{2,1,0:T(8,128)(2,1)S(1)} %add_convert_fusion), channel_id=1, source_target_pairs={{16,0},{48,32},{80,64},{112,96},{144,128},{176,160},{208,192},{240... | collective-permute-start | bytes 3145736 | tf_op jit(solution)/shard_map/ppermute | solution.py:309
  101.9 18.4 %copy-start.3 = (f32[2,2048,128]{2,1,0:T(8,128)S(1)}, f32[2,2048,128]{2,1,0:T(8,128)}, u32[]{:S(2)}) copy-start(f32[2,2048,128]{2,1,0:T(8,128)} %select_add_fusion.refs_5_) | copy-start | bytes 6291460

commit v4 on v3

--- a/solution.py
+++ b/solution.py
@@ -43,7 +43,7 @@
 
 
 def pack_kernel(q, k, v, g, out):
-    for m in range(PARTS):
+    for m in range(QUAD):
         wide, thin = slice(m * WIDE, (m + 1) * WIDE), slice(m * HD, (m + 1) * HD)
         out[m, :, :WIDE] = q[:, wide]
         out[m, :, WIDE : 2 * WIDE] = g[:, wide]
@@ -52,11 +52,13 @@
 
 
 def pack(q, k, v, g):
-    vmem = pl.BlockSpec(memory_space=pltpu.VMEM)
+    wide = pl.BlockSpec((ROWS, QUAD * WIDE), lambda n: (0, n))
+    thin = pl.BlockSpec((ROWS, QUAD * HD), lambda n: (0, n))
     return pl.pallas_call(
         pack_kernel,
-        in_specs=[vmem] * 4,
-        out_specs=vmem,
+        grid=(PARTS // QUAD,),
+        in_specs=[wide, thin, thin, wide],
+        out_specs=pl.BlockSpec((QUAD, ROWS, SEND), lambda n: (n, 0, 0)),
         out_shape=jax.ShapeDtypeStruct((PARTS, ROWS, SEND), BF16),
         name="pack",
     )(q, k, v, g)
@@ -325,7 +327,7 @@
     back_near, own_grads, lead_grads = attend(
         "near", 0, scalars, rows, (pk, pv), leads, (own_grads, lead_grads)
     )
-    back = [swap(x, QUAD + n) for n, x in enumerate(back)]
+    back = [swap(x, QUAD + n) if n < 3 else x for n, x in enumerate(back)]
     quads = [list(range(n, n + QUAD)) for n in range(0, PARTS, QUAD)]
     back_near = lax.all_to_all(
         back_near, "mp", split_axis=0, concat_axis=0, axis_index_groups=quads, tiled=True
@@ -334,6 +336,8 @@
     lead_grads, *back[:2] = lax.optimization_barrier((lead_grads, *back[:2]))
     near_grads = send(lead_grads, (1, 0), (3, 2))
     near_sum = (lead_grads + near_grads).astype(BF16)
+    near_sum, back[3] = lax.optimization_barrier((near_sum, back[3]))
+    back[3] = swap(back[3], QUAD + 3)
     far_grads = send(near_sum, (2, 0))
     near_sum, near_grads = lax.optimization_barrier((near_sum, near_grads))
     base = own_grads + jnp.where(leader, lead_grads + near_grads, 0.0)

time: 123 us -> 123 us (level)
    ppermute x4, waiting for transfers between devices: 16.9 us -> 12.2 us  [swap(): return lax.ppermute(x, 'mp', [(i, i ^ p) for i in range(PARTS)])]
    all_to_all x1, waiting for transfers between devices: 1.84 us -> 6.52 us  [local(): lax.all_to_all(back_near, 'mp', split_axis=0, concat_axis=0, axis_index_g...]
    unnamed x17 -> x19, local copies, waits for them, and re-layouts: 1.85 us -> 2.51 us
  transfers between devices with their start and end apart: 10 -> 10, of which waited for: 6 -> 5; matrix products, arithmetic and copies ran while one was open for 5% -> 5% of each run, Pallas kernels for 13% -> 13%
where the time goes in v4:
time: 123 us; the launch traced here: 122 us
  waiting for transfers between devices  51 us (41%)
  Pallas kernels  31.8 us (26%)
  starting transfers between devices  28.7 us (23%)
  other arithmetic  6.77 us (6%)
  local copies, waits for them, and re-layouts  3.34 us (3%)
    pallas_call x2, Pallas kernels, attend(): pl.pallas_call(functools.partial(attend_kernel, far, len(chain) > 0), gri...  26.6 us
    ppermute x4, waiting for transfers between devices, send(): lax.ppermute(x, 'dp', [(REACH * n + a, REACH * n + b) for n in range(grou...  19.1 us
    all_to_all x1, waiting for transfers between devices, local(): rows = lax.all_to_all(rows, 'mp', split_axis=0, concat_axis=0, tiled=True)  13.2 us
    ppermute x4, waiting for transfers between devices, swap(): return lax.ppermute(x, 'mp', [(i, i ^ p) for i in range(PARTS)])  12.2 us
    all_to_all x1, starting transfers between devices, local(): rows = lax.all_to_all(rows, 'mp', split_axis=0, concat_axis=0, tiled=True)  8.15 us
    ppermute x4, starting transfers between devices, swap(): return lax.ppermute(x, 'mp', [(i, i ^ p) for i in range(PARTS)])  8.11 us
    all_to_all x1, waiting for transfers between devices, local(): lax.all_to_all(back_near, 'mp', split_axis=0, concat_axis=0, axis_index_g...  6.52 us
    all_to_all x1, starting transfers between devices, local(): lax.all_to_all(back_near, 'mp', split_axis=0, concat_axis=0, axis_index_g...  6.25 us
  transfers between devices with their start and end apart: 10, of which 5 were waited for; matrix products, arithmetic and copies ran while one was open for 5% of the time, Pallas kernels for 13%

profile of v4, /device:TPU:61, one launch (start us, length us, event | category | flops | bytes accessed | tf_op | source)
XLA Modules:
  0.0 122.4 jit_solution(11247182663193289829)
XLA Ops:
  0.6 2.4 %pack.1 = bf16[8,64,1536]{2,1,0:T(8,128)(2,1)} custom-call(bf16[64,5120]{1,0:T(8,128)(2,1)} %q.1, bf16[64,1024]{1,0:T(8,128)(2,1)} %k.1, bf16[64,1024]{1,0:T(8,128)(2,1)} %v.1, bf16[64,5120]{1,0:T(8,128)(2,1)} %g.1), custom_call_target="tpu_custom_call" | custom-call | tf_op jit(solution)/shard_map/pack/pallas_call | solution.py:57
  3.0 0.0 copy-start.4
  3.0 0.0 copy-start.5
  3.0 8.1 %all-to-all-start = ((bf16[8,64,1536]{2,1,0:T(8,128)(2,1)}), bf16[8,64,1536]{2,1,0:T(8,128)(2,1)}, u32[]{:S(2)}, u32[]{:S(2)}) async-start(bf16[8,64,1536]{2,1,0:T(8,128)(2,1)} %pack.1), calls=%async_computation | async-start | bytes 3145728 | tf_op jit(solution)/shard_map/all_to_all | solution.py:325
  11.2 0.0 copy-done.4
  11.2 0.8 constant_dynamic-update-slice_fusion.1
  12.0 0.0 copy-done.5
  12.0 0.8 constant_dynamic-update-slice_fusion
  12.9 0.7 collective-permute-start
  13.6 0.0 collective-permute-done.refs_3_
  13.6 0.0 copy-start.1
  13.6 1.0 copy-done.1
  14.6 0.1 broadcast_select_fusion
  14.7 1.3 %collective-permute-start.1 = (bf16[2,2048,128]{2,1,0:T(8,128)(2,1)S(1)}, bf16[2,2048,128]{2,1,0:T(8,128)(2,1)}, u32[]{:S(2)}, u32[]{:S(2)}) collective-permute-start(bf16[2,2048,128]{2,1,0:T(8,128)(2,1)S(1)} %broadcast_select_fusion), channel_id=1, source_target_pairs={{0,8},{16,24},{32,40},{48,56},{64,72},{80,88},{96,104},{112,120},{... | collective-permute-start | bytes 3145736 | tf_op jit(solution)/shard_map/ppermute | solution.py:311
  16.0 0.6 pad_add_fusion.ids
  16.6 19.1 %collective-permute-done.1.refs_4_ = bf16[2,2048,128]{2,1,0:T(8,128)(2,1)} collective-permute-done((bf16[2,2048,128]{2,1,0:T(8,128)(2,1)S(1)}, bf16[2,2048,128]{2,1,0:T(8,128)(2,1)}, u32[]{:S(2)}, u32[]{:S(2)}) %collective-permute-start.1) | collective-permute-done | bytes 1048608 | tf_op jit(solution)/shard_map/ppermute | solution.py:311
  35.6 13.2 %all-to-all-done.refs_0_ = bf16[8,64,1536]{2,1,0:T(8,128)(2,1)} async-done(((bf16[8,64,1536]{2,1,0:T(8,128)(2,1)}), bf16[8,64,1536]{2,1,0:T(8,128)(2,1)}, u32[]{:S(2)}, u32[]{:S(2)}) %all-to-all-start) | async-done | bytes 1572896 | tf_op jit(solution)/shard_map/all_to_all | solution.py:325
  48.9 13.4 %far.1 = (bf16[64,1536]{1,0:T(8,128)(2,1)}, bf16[64,1536]{1,0:T(8,128)(2,1)}, bf16[64,1536]{1,0:T(8,128)(2,1)}, bf16[64,1536]{1,0:T(8,128)(2,1)}, f32[2,2048,128]{2,1,0:T(8,128)}, /*index=5*/f32[2,2048,128]{2,1,0:T(8,128)}) custom-call(s32[2]{0:T(128)} %pad_add_fusion.ids, s32[2]{0:T(128)} %prompt_of.3, s32[2]{0:T(128)} %lengths.3, ...), custom_call_target="tpu_custom_call" | custom-call | flops 1048576 | bytes 65536 | tf_op jit(solution)/shard_map/far/pallas_call | solution.py:267
  62.3 0.5 collective-permute-start.2
  62.9 4.4 %collective-permute-start.3 = (bf16[64,1536]{1,0:T(8,128)(2,1)}, bf16[64,1536]{1,0:T(8,128)(2,1)S(1)}, u32[]{:S(2)}, u32[]{:S(2)}) collective-permute-start(bf16[64,1536]{1,0:T(8,128)(2,1)} %get-tuple-element.35), channel_id=1, source_target_pairs={{0,5},{1,4},{2,7},{3,6},{4,1},{5,0},{6,3},{7,2},{8,13},{9,12},{10,... | collective-permute-start | bytes 589832 | tf_op jit(solution)/shard_map/ppermute | solution.py:316
  67.3 13.2 %near.1 = (bf16[4,64,1536]{2,1,0:T(8,128)(2,1)}, f32[2,2048,128]{2,1,0:T(8,128)}, f32[2,2048,128]{2,1,0:T(8,128)}) custom-call(s32[2]{0:T(128)} %pad_add_fusion.ids, s32[2]{0:T(128)} %prompt_of.3, s32[2]{0:T(128)} %lengths.3, bf16[8,64,1536]{2,1,0:T(8,128)(2,1)} %all-to-all-done.refs_0_, ...), custom_call_target="tpu_custom_call", output_to_operand_aliasing={{1}: (8, {}), {2}: (9, {})} | custom-call | flops 1048576 | bytes 65536 | tf_op jit(solution)/shard_map/near/pallas_call | solution.py:267
  80.5 0.0 collective-permute-done.2.refs_0_
  80.5 0.0 copy-start.6
  80.5 3.1 %collective-permute-done.3.refs_1_ = bf16[64,1536]{1,0:T(8,128)(2,1)S(1)} collective-permute-done((bf16[64,1536]{1,0:T(8,128)(2,1)}, bf16[64,1536]{1,0:T(8,128)(2,1)S(1)}, u32[]{:S(2)}, u32[]{:S(2)}) %collective-permute-start.3) | collective-permute-done | bytes 196640 | tf_op jit(solution)/shard_map/ppermute | solution.py:316
  83.6 0.0 copy-start.7
  83.6 2.5 %collective-permute-start.5 = (f32[2,2048,128]{2,1,0:T(8,128)}, f32[2,2048,128]{2,1,0:T(8,128)S(1)}, u32[]{:S(2)}, u32[]{:S(2)}) collective-permute-start(f32[2,2048,128]{2,1,0:T(8,128)} %get-tuple-element.39), channel_id=1, source_target_pairs={{8,0},{24,16},{40,32},{56,48},{72,64},{88,80},{104,96},{120,112},{... | collective-permute-start | bytes 6291464 | tf_op jit(solution)/shard_map/ppermute | solution.py:311
  86.1 6.2 %all-to-all-start.1 = ((bf16[4,64,1536]{2,1,0:T(8,128)(2,1)}), bf16[4,64,1536]{2,1,0:T(8,128)(2,1)}, u32[]{:S(2)}, u32[]{:S(2)}) async-start(bf16[4,64,1536]{2,1,0:T(8,128)(2,1)} %get-tuple-element.42), calls=%async_computation.1 | async-start | bytes 1572864 | tf_op jit(solution)/shard_map/all_to_all | solution.py:332
  92.4 0.0 copy-start
  92.4 0.0 copy-start.2
  92.4 0.6 collective-permute-start.4
  93.0 0.0 collective-permute-done.5
  93.0 2.1 %add_convert_fusion = bf16[2,2048,128]{2,1,0:T(8,128)(2,1)S(1)} fusion(f32[2,2048,128]{2,1,0:T(8,128)} %get-tuple-element.39, f32[2,2048,128]{2,1,0:T(8,128)S(1)} %collective-permute-done.5), kind=kLoop, calls=%fused_computation.1 | loop fusion | flops 1048576 | bytes 5242880 | tf_op jit(solution)/shard_map/convert_element_type | solution.py:338
  95.0 0.0 copy-done.6
  95.0 0.0 copy-done.7
  95.1 1.7 %collective-permute-start.7 = (bf16[2,2048,128]{2,1,0:T(8,128)(2,1)S(1)}, bf16[2,2048,128]{2,1,0:T(8,128)(2,1)}, u32[]{:S(2)}, u32[]{:S(2)}) collective-permute-start(bf16[2,2048,128]{2,1,0:T(8,128)(2,1)S(1)} %add_convert_fusion), channel_id=1, source_target_pairs={{16,0},{48,32},{80,64},{112,96},{144,128},{176,160},{208,192},{240... | collective-permute-start | bytes 3145736 | tf_op jit(solution)/shard_map/ppermute | solution.py:311
  96.7 2.6 %collective-permute-start.6 = (bf16[64,1536]{1,0:T(8,128)(2,1)}, bf16[64,1536]{1,0:T(8,128)(2,1)S(1)}, u32[]{:S(2)}, u32[]{:S(2)}) collective-permute-start(bf16[64,1536]{1,0:T(8,128)(2,1)} %get-tuple-element.41), channel_id=1, source_target_pairs={{0,7},{1,6},{2,5},{3,4},{4,3},{5,2},{6,1},{7,0},{8,15},{9,14},{10,... | collective-permute-start | bytes 589832 | tf_op jit(solution)/shard_map/ppermute | solution.py:316
  99.3 0.0 copy-done
  99.3 0.0 copy-done.2
  99.3 1.6 %select_add_fusion.refs_5_ = f32[2,2048,128]{2,1,0:T(8,128)} fusion(f32[2,2048,128]{2,1,0:T(8,128)S(1)} %copy-done.2, f32[2,2048,128]{2,1,0:T(8,128)S(1)} %copy-done, f32[2,2048,128]{2,1,0:T(8,128)S(1)} %collective-permute-done.5, pred[]{:T(512)S(6)} %eq.5), kind=kLoop, calls=%fused_computation | loop fusion | flops 1572864 | bytes 8388609 | tf_op jit(solution)/shard_map/add | solution.py:343
  101.0 0.0 copy-start.3
  101.0 9.1 %collective-permute-done.4.refs_2_ = bf16[64,1536]{1,0:T(8,128)(2,1)} collective-permute-done((bf16[64,1536]{1,0:T(8,128)(2,1)}, bf16[64,1536]{1,0:T(8,128)(2,1)}, u32[]{:S(2)}, u32[]{:S(2)}) %collective-permute-start.4) | collective-permute-done | bytes 196640 | tf_op jit(solution)/shard_map/ppermute | solution.py:316
  110.1 6.5 %all-to-all-done.1.refs_4_ = bf16[4,64,1536]{2,1,0:T(8,128)(2,1)} async-done(((bf16[4,64,1536]{2,1,0:T(8,128)(2,1)}), bf16[4,64,1536]{2,1,0:T(8,128)(2,1)}, u32[]{:S(2)}, u32[]{:S(2)}) %all-to-all-start.1) | async-done | bytes 786464 | tf_op jit(solution)/shard_map/all_to_all | solution.py:332
  116.6 0.0 collective-permute-done.6.refs_3_
  116.6 0.0 copy-start.8
  116.6 0.7 copy-done.8
  117.2 2.8 %unpack.1 = (bf16[64,5120]{1,0:T(8,128)(2,1)}, bf16[64,5120]{1,0:T(8,128)(2,1)}, bf16[64,1024]{1,0:T(8,128)(2,1)}, bf16[64,1024]{1,0:T(8,128)(2,1)}) custom-call(s32[2]{0:T(128)} %pad_add_fusion.ids, bf16[64,1536]{1,0:T(8,128)(2,1)} %copy-done.6, bf16[64,1536]{1,0:T(8,128)(2,1)} %copy-done.7, bf16[64,1536]{1,0:T(8,128)(2,1)} %collective-permute-done.4.refs_2_, ...), custom_call_target="tpu_custom_call" | custom-call | flops 68719476736 | bytes 4194304 | tf_op jit(solution)/shard_map/unpack/pallas_call | solution.py:85
  120.0 0.0 collective-permute-done.7
  120.0 0.0 copy-done.3
  120.0 2.4 %fusion = (bf16[1,2048,128]{2,1,0:T(8,128)(2,1)}, bf16[1,2048,128]{2,1,0:T(8,128)(2,1)}) fusion(f32[2,2048,128]{2,1,0:T(8,128)S(1)} %copy-done.3, bf16[2,2048,128]{2,1,0:T(8,128)(2,1)} %collective-permute-done.7), kind=kLoop, calls=%fused_computation.3 | loop fusion | flops 1572864 | bytes 4194304 | tf_op jit(solution)/shard_map/convert_element_type | solution.py:345
Async XLA Ops:
  3.0 8.2 %copy-start.4 = (bf16[1,2048,128]{2,1,0:T(8,128)(2,1)S(1)}, bf16[1,2048,128]{2,1,0:T(8,128)(2,1)}, u32[]{:S(2)}) copy-start(bf16[1,2048,128]{2,1,0:T(8,128)(2,1)} %param.11) | copy-start | bytes 1572868
  3.0 9.0 %copy-start.5 = (bf16[1,2048,128]{2,1,0:T(8,128)(2,1)S(1)}, bf16[1,2048,128]{2,1,0:T(8,128)(2,1)}, u32[]{:S(2)}) copy-start(bf16[1,2048,128]{2,1,0:T(8,128)(2,1)} %param.12) | copy-start | bytes 1572868
  3.0 45.9 %all-to-all-start = ((bf16[8,64,1536]{2,1,0:T(8,128)(2,1)}), bf16[8,64,1536]{2,1,0:T(8,128)(2,1)}, u32[]{:S(2)}, u32[]{:S(2)}) async-start(bf16[8,64,1536]{2,1,0:T(8,128)(2,1)} %pack.1), calls=%async_computation | async-start | bytes 3145728 | tf_op jit(solution)/shard_map/all_to_all | solution.py:325
  12.9 0.7 collective-permute-start
  13.6 1.0 copy-start.1
  14.7 20.9 %collective-permute-start.1 = (bf16[2,2048,128]{2,1,0:T(8,128)(2,1)S(1)}, bf16[2,2048,128]{2,1,0:T(8,128)(2,1)}, u32[]{:S(2)}, u32[]{:S(2)}) collective-permute-start(bf16[2,2048,128]{2,1,0:T(8,128)(2,1)S(1)} %broadcast_select_fusion), channel_id=1, source_target_pairs={{0,8},{16,24},{32,40},{48,56},{64,72},{80,88},{96,104},{112,120},{... | collective-permute-start | bytes 3145736 | tf_op jit(solution)/shard_map/ppermute | solution.py:311
  62.3 18.2 %collective-permute-start.2 = (bf16[64,1536]{1,0:T(8,128)(2,1)}, bf16[64,1536]{1,0:T(8,128)(2,1)S(1)}, u32[]{:S(2)}, u32[]{:S(2)}) collective-permute-start(bf16[64,1536]{1,0:T(8,128)(2,1)} %get-tuple-element.34), channel_id=1, source_target_pairs={{0,4},{1,5},{2,6},{3,7},{4,0},{5,1},{6,2},{7,3},{8,12},{9,13},{10,... | collective-permute-start | bytes 589832 | tf_op jit(solution)/shard_map/ppermute | solution.py:316
  62.9 20.7 %collective-permute-start.3 = (bf16[64,1536]{1,0:T(8,128)(2,1)}, bf16[64,1536]{1,0:T(8,128)(2,1)S(1)}, u32[]{:S(2)}, u32[]{:S(2)}) collective-permute-start(bf16[64,1536]{1,0:T(8,128)(2,1)} %get-tuple-element.35), channel_id=1, source_target_pairs={{0,5},{1,4},{2,7},{3,6},{4,1},{5,0},{6,3},{7,2},{8,13},{9,12},{10,... | collective-permute-start | bytes 589832 | tf_op jit(solution)/shard_map/ppermute | solution.py:316
  80.5 14.6 %copy-start.6 = (bf16[64,1536]{1,0:T(8,128)(2,1)}, bf16[64,1536]{1,0:T(8,128)(2,1)S(1)}, u32[]{:S(2)}) copy-start(bf16[64,1536]{1,0:T(8,128)(2,1)S(1)} %collective-permute-done.2.refs_0_) | copy-start | bytes 589828
  83.6 11.4 %copy-start.7 = (bf16[64,1536]{1,0:T(8,128)(2,1)}, bf16[64,1536]{1,0:T(8,128)(2,1)S(1)}, u32[]{:S(2)}) copy-start(bf16[64,1536]{1,0:T(8,128)(2,1)S(1)} %collective-permute-done.3.refs_1_) | copy-start | bytes 589828
  83.6 9.3 %collective-permute-start.5 = (f32[2,2048,128]{2,1,0:T(8,128)}, f32[2,2048,128]{2,1,0:T(8,128)S(1)}, u32[]{:S(2)}, u32[]{:S(2)}) collective-permute-start(f32[2,2048,128]{2,1,0:T(8,128)} %get-tuple-element.39), channel_id=1, source_target_pairs={{8,0},{24,16},{40,32},{56,48},{72,64},{88,80},{104,96},{120,112},{... | collective-permute-start | bytes 6291464 | tf_op jit(solution)/shard_map/ppermute | solution.py:311
  86.1 30.4 %all-to-all-start.1 = ((bf16[4,64,1536]{2,1,0:T(8,128)(2,1)}), bf16[4,64,1536]{2,1,0:T(8,128)(2,1)}, u32[]{:S(2)}, u32[]{:S(2)}) async-start(bf16[4,64,1536]{2,1,0:T(8,128)(2,1)} %get-tuple-element.42), calls=%async_computation.1 | async-start | bytes 1572864 | tf_op jit(solution)/shard_map/all_to_all | solution.py:332
  92.4 7.0 %copy-start = (f32[2,2048,128]{2,1,0:T(8,128)S(1)}, f32[2,2048,128]{2,1,0:T(8,128)}, u32[]{:S(2)}) copy-start(f32[2,2048,128]{2,1,0:T(8,128)} %get-tuple-element.39) | copy-start | bytes 6291460
  92.4 7.0 %copy-start.2 = (f32[2,2048,128]{2,1,0:T(8,128)S(1)}, f32[2,2048,128]{2,1,0:T(8,128)}, u32[]{:S(2)}) copy-start(f32[2,2048,128]{2,1,0:T(8,128)} %get-tuple-element.43) | copy-start | bytes 6291460
  92.4 17.7 %collective-permute-start.4 = (bf16[64,1536]{1,0:T(8,128)(2,1)}, bf16[64,1536]{1,0:T(8,128)(2,1)}, u32[]{:S(2)}, u32[]{:S(2)}) collective-permute-start(bf16[64,1536]{1,0:T(8,128)(2,1)} %get-tuple-element.38), channel_id=1, source_target_pairs={{0,6},{1,7},{2,4},{3,5},{4,2},{5,3},{6,0},{7,1},{8,14},{9,15},{10,... | collective-permute-start | bytes 589832 | tf_op jit(solution)/shard_map/ppermute | solution.py:316
  95.1 25.0 %collective-permute-start.7 = (bf16[2,2048,128]{2,1,0:T(8,128)(2,1)S(1)}, bf16[2,2048,128]{2,1,0:T(8,128)(2,1)}, u32[]{:S(2)}, u32[]{:S(2)}) collective-permute-start(bf16[2,2048,128]{2,1,0:T(8,128)(2,1)S(1)} %add_convert_fusion), channel_id=1, source_target_pairs={{16,0},{48,32},{80,64},{112,96},{144,128},{176,160},{208,192},{240... | collective-permute-start | bytes 3145736 | tf_op jit(solution)/shard_map/ppermute | solution.py:311
  96.7 19.8 %collective-permute-start.6 = (bf16[64,1536]{1,0:T(8,128)(2,1)}, bf16[64,1536]{1,0:T(8,128)(2,1)S(1)}, u32[]{:S(2)}, u32[]{:S(2)}) collective-permute-start(bf16[64,1536]{1,0:T(8,128)(2,1)} %get-tuple-element.41), channel_id=1, source_target_pairs={{0,7},{1,6},{2,5},{3,4},{4,3},{5,2},{6,1},{7,0},{8,15},{9,14},{10,... | collective-permute-start | bytes 589832 | tf_op jit(solution)/shard_map/ppermute | solution.py:316
  101.0 19.1 %copy-start.3 = (f32[2,2048,128]{2,1,0:T(8,128)S(1)}, f32[2,2048,128]{2,1,0:T(8,128)}, u32[]{:S(2)}) copy-start(f32[2,2048,128]{2,1,0:T(8,128)} %select_add_fusion.refs_5_) | copy-start | bytes 6291460
  116.6 0.7 copy-start.8
